TPU v7x, 32 devices: a whole 2x2x4 slice. The times are simulated.
32 devices in a mesh: fsdp: 4 (over y, core), ctx: 4 (over z), tp: 2 (over x).
Axes of the slice: x: 2, y: 2, z: 4, core: 2. Of those that a mesh axis runs over, the one named last changes fastest.
Arguments:
- inputs: bfloat16 [4, 1024, 1536], P('fsdp', 'ctx'), may hold values from -6 to 6
- cotangent: bfloat16 [4, 1024, 1536], P('fsdp', 'ctx'), may hold values from -6 to 6
- doc_bounds: int32 [4, 2], P('fsdp'), may hold values from 1 to 1023, as said below
- attn_gain: bfloat16 [1536], P(('fsdp', 'ctx')), may hold values from 0.5 to 1.5
- w_query: bfloat16 [1536, 1536], P(('fsdp', 'ctx'), 'tp'), may hold values from -0.15625 to 0.15625
- w_key: bfloat16 [1536, 512], P(('fsdp', 'ctx'), 'tp'), may hold values from -0.15625 to 0.15625
- w_value: bfloat16 [1536, 512], P(('fsdp', 'ctx'), 'tp'), may hold values from -0.15625 to 0.15625
- w_output: bfloat16 [1536, 1536], P('tp', ('fsdp', 'ctx')), may hold values from -2.5 to 2.5
- query_gain: bfloat16 [64], P(('fsdp', 'ctx')), may hold values from 0.099609375 to 1.8984375
- key_gain: bfloat16 [64], P(('fsdp', 'ctx')), may hold values from 0.099609375 to 1.8984375
- ffn_gain: bfloat16 [1536], P(('fsdp', 'ctx')), may hold values from 0.5 to 1.5
- w_gate: bfloat16 [1536, 6912], P(('fsdp', 'ctx'), 'tp'), may hold values from -0.15625 to 0.15625
- w_up: bfloat16 [1536, 6912], P(('fsdp', 'ctx'), 'tp'), may hold values from -0.15625 to 0.15625
- w_down: bfloat16 [6912, 1536], P('tp', ('fsdp', 'ctx')), may hold values from -0.078125 to 0.078125
Outputs:
- result: bfloat16 [4, 1024, 1536], P('fsdp', 'ctx')
- grad_inputs: float32 [4, 1024, 1536], P('fsdp', 'ctx')
- grad_attn_gain: float32 [1536], P(('fsdp', 'ctx'))
- grad_query: float32 [1536, 1536], P(('fsdp', 'ctx'), 'tp')
- grad_key: float32 [1536, 512], P(('fsdp', 'ctx'), 'tp')
- grad_value: float32 [1536, 512], P(('fsdp', 'ctx'), 'tp')
- grad_output: float32 [1536, 1536], P('tp', ('fsdp', 'ctx'))
- grad_query_gain: float32 [64], P(('fsdp', 'ctx'))
- grad_key_gain: float32 [64], P(('fsdp', 'ctx'))
- grad_ffn_gain: float32 [1536], P(('fsdp', 'ctx'))
- grad_gate: float32 [1536, 6912], P(('fsdp', 'ctx'), 'tp')
- grad_up: float32 [1536, 6912], P(('fsdp', 'ctx'), 'tp')
- grad_down: float32 [6912, 1536], P('tp', ('fsdp', 'ctx'))
Inputs may be any that keep to these rules, and one draw needn't show every extreme that they name: Each sequence holds three documents: the second begins at doc_bounds[s,0], one of the indices 1 to 255, the third at doc_bounds[s,1], one of the indices 1024 - 255 to 1023.
All inputs are finite; a program needn't handle non-finite values.
Results may differ from a plain program's by a relative error of at most 0.02.
Values may be sent and summed in bfloat16 or wider, within the bound.
No kernel may reach another device: no remote copies, remote signals or barrier semaphores. Data moves between devices by JAX's collectives and lax.ppermute only.
A program may use at most 192 MiB of HBM per device.

v0:
```python
import jax
import jax.numpy as jnp
from jax import lax
from jax.sharding import PartitionSpec as P

HQ = 24
HK = 8
HEAD = 64


EPS = 1e-05
THETA = 1000000.0
NEG = -1e30


def inverse_rms(values):
    return lax.rsqrt(jnp.mean(values * values, axis=-1, keepdims=True) + EPS)


def rotate(values, cosine, sine):
    half = values.shape[-1] // 2
    front = values[..., :half]
    back = values[..., half:]
    return jnp.concatenate([front * cosine - back * sine, back * cosine + front * sine], axis=-1)


def unrotate(grads, cosine, sine):
    half = grads.shape[-1] // 2
    front = grads[..., :half]
    back = grads[..., half:]
    return jnp.concatenate([front * cosine + back * sine, back * cosine - front * sine], axis=-1)


def norm_back(values, inverse, gain, grads):
    scaled = grads * gain
    return inverse * scaled - values * (inverse * inverse * inverse) * jnp.mean(
        scaled * values, axis=-1, keepdims=True
    )


def contract_rows(left, right):
    return lax.dot_general(
        left, right, (((0,), (0,)), ((), ())), preferred_element_type=jnp.float32
    )


def contract_cols(left, right):
    return lax.dot_general(
        left, right, (((1,), (1,)), ((), ())), preferred_element_type=jnp.float32
    )


def document(index, bounds):
    return (index >= bounds[0]).astype(jnp.int32) + (index >= bounds[1]).astype(jnp.int32)


def doc_position(index, bounds):
    begin = jnp.where(index >= bounds[1], bounds[1], jnp.where(index >= bounds[0], bounds[0], 0))
    return index - begin


def tables(where_in):
    freq = THETA ** (-(jnp.arange(HEAD // 2, dtype=jnp.float32) * 2.0 / HEAD))
    angle = where_in.astype(jnp.float32)[:, None] * freq[None, :]
    return (jnp.cos(angle)[:, None, :], jnp.sin(angle)[:, None, :])


def keep_state(current):
    return current


def body(
    inputs,
    cotangent,
    doc_bounds,
    attn_gain,
    w_query,
    w_key,
    w_value,
    w_output,
    query_gain,
    key_gain,
    ffn_gain,
    w_gate,
    w_up,
    w_down,
):
    gain_attn, full_query, full_key, full_value, full_output, gain_query, gain_key = (
        lax.all_gather(attn_gain, ("fsdp", "ctx"), axis=0, tiled=True),
        lax.all_gather(w_query, ("fsdp", "ctx"), axis=0, tiled=True),
        lax.all_gather(w_key, ("fsdp", "ctx"), axis=0, tiled=True),
        lax.all_gather(w_value, ("fsdp", "ctx"), axis=0, tiled=True),
        lax.all_gather(w_output, ("fsdp", "ctx"), axis=1, tiled=True),
        lax.all_gather(query_gain, ("fsdp", "ctx"), axis=0, tiled=True),
        lax.all_gather(key_gain, ("fsdp", "ctx"), axis=0, tiled=True),
    )
    gain_ffn, full_gate, full_up, full_down = (
        lax.all_gather(ffn_gain, ("fsdp", "ctx"), axis=0, tiled=True),
        lax.all_gather(w_gate, ("fsdp", "ctx"), axis=0, tiled=True),
        lax.all_gather(w_up, ("fsdp", "ctx"), axis=0, tiled=True),
        lax.all_gather(w_down, ("fsdp", "ctx"), axis=1, tiled=True),
    )
    tensor = lax.axis_size("tp")
    query_heads = HQ // tensor
    key_heads = HK // tensor
    groups = HQ // HK
    kv_width = key_heads * HEAD
    tokens = inputs[0].astype(jnp.float32)
    rows = tokens.shape[0]
    length = rows * lax.axis_size("ctx")
    first = lax.axis_index("ctx") * rows
    last_row = first + rows - 1
    bounds = doc_bounds[0]
    row_index = first + jnp.arange(rows, dtype=jnp.int32)
    row_docs = document(row_index, bounds)
    cosine, sine = tables(doc_position(row_index, bounds))
    scale = HEAD ** (-0.5)
    first_inv = inverse_rms(tokens)
    normed = (tokens * first_inv * gain_attn.astype(jnp.float32)).astype(jnp.bfloat16)
    queries = jnp.dot(normed, full_query, preferred_element_type=jnp.float32).reshape(
        rows, query_heads, HEAD
    )
    keys = jnp.dot(normed, full_key, preferred_element_type=jnp.float32).reshape(
        rows, key_heads, HEAD
    )
    values = jnp.dot(normed, full_value, preferred_element_type=jnp.float32).astype(jnp.bfloat16)
    query_inv = inverse_rms(queries)
    key_inv = inverse_rms(keys)
    query_rot = (
        rotate(queries * query_inv * gain_query.astype(jnp.float32), cosine, sine)
        .astype(jnp.bfloat16)
        .reshape(rows, key_heads, groups, HEAD)
    )
    key_rot = (
        rotate(keys * key_inv * gain_key.astype(jnp.float32), cosine, sine)
        .astype(jnp.bfloat16)
        .reshape(rows, kv_width)
    )
    all_keys, all_values = (
        lax.all_gather(key_rot, "ctx", axis=0, tiled=True),
        lax.all_gather(values, "ctx", axis=0, tiled=True),
    )
    block = 512
    block_count = length // block
    block_ids = jnp.arange(block_count, dtype=jnp.int32)

    def block_scores(block_id):
        start = block_id * block
        key_block = lax.dynamic_slice_in_dim(all_keys, start, block, 0).reshape(
            block, key_heads, HEAD
        )
        value_block = lax.dynamic_slice_in_dim(all_values, start, block, 0).reshape(
            block, key_heads, HEAD
        )
        key_index = start + jnp.arange(block, dtype=jnp.int32)
        allowed = (key_index[None, :] <= row_index[:, None]) & (
            document(key_index, bounds)[None, :] == row_docs[:, None]
        )
        scores = (
            jnp.einsum("qkge,tke->kgqt", query_rot, key_block, preferred_element_type=jnp.float32)
            * scale
        )
        return (key_block, value_block, allowed, scores)

    def stats_step(state, block_id):

        def stats_work(current):
            top, total = current
            scores_all = block_scores(block_id)
            allowed = scores_all[2]
            scores = scores_all[3]
            new_top = jnp.maximum(top, jnp.max(jnp.where(allowed, scores, NEG), axis=-1))
            weights = jnp.where(allowed, jnp.exp(scores - new_top[..., None]), 0.0)
            return (new_top, total * jnp.exp(top - new_top) + jnp.sum(weights, axis=-1))

        return (lax.cond(block_id * block <= last_row, stats_work, keep_state, state), None)

    top_start = jnp.full((key_heads, groups, rows), NEG, jnp.float32)
    total_start = jnp.zeros((key_heads, groups, rows), jnp.float32)
    (top, total), _ = lax.scan(stats_step, (top_start, total_start), block_ids)
    log_total = top + jnp.log(total)

    def value_step(accum, block_id):

        def value_work(current):
            _, value_block, allowed, scores = block_scores(block_id)
            probs = jnp.where(allowed, jnp.exp(scores - log_total[..., None]), 0.0).astype(
                jnp.bfloat16
            )
            return current + jnp.einsum(
                "kgqt,tke->qkge", probs, value_block, preferred_element_type=jnp.float32
            )

        return (lax.cond(block_id * block <= last_row, value_work, keep_state, accum), None)

    mixed, _ = lax.scan(
        value_step, jnp.zeros((rows, key_heads, groups, HEAD), jnp.float32), block_ids
    )
    mixed_low = mixed.reshape(rows, query_heads * HEAD).astype(jnp.bfloat16)
    branch = lax.psum(
        jnp.dot(mixed_low, full_output, preferred_element_type=jnp.float32).astype(jnp.bfloat16),
        "tp",
    ).astype(jnp.float32)
    hidden = tokens + branch
    second_inv = inverse_rms(hidden)
    hidden_normed = (hidden * second_inv * gain_ffn.astype(jnp.float32)).astype(jnp.bfloat16)
    gate = jnp.dot(hidden_normed, full_gate, preferred_element_type=jnp.float32)
    upward = jnp.dot(hidden_normed, full_up, preferred_element_type=jnp.float32)
    sigma = jax.nn.sigmoid(gate)
    active = gate * sigma
    middle = (active * upward).astype(jnp.bfloat16)
    feed = lax.psum(
        jnp.dot(middle, full_down, preferred_element_type=jnp.float32).astype(jnp.bfloat16), "tp"
    ).astype(jnp.float32)
    result = (hidden + feed).astype(jnp.bfloat16)[None]
    gain_ffn, full_gate, full_up, full_down = (
        lax.all_gather(ffn_gain, ("fsdp", "ctx"), axis=0, tiled=True),
        lax.all_gather(w_gate, ("fsdp", "ctx"), axis=0, tiled=True),
        lax.all_gather(w_up, ("fsdp", "ctx"), axis=0, tiled=True),
        lax.all_gather(w_down, ("fsdp", "ctx"), axis=1, tiled=True),
    )
    pulled = cotangent[0]
    grad_down = contract_rows(middle, pulled)
    grad_middle = contract_cols(pulled, full_down)
    grad_gate_low = (grad_middle * upward * sigma * (1.0 + gate * (1.0 - sigma))).astype(
        jnp.bfloat16
    )
    grad_up_low = (grad_middle * active).astype(jnp.bfloat16)
    grad_gate = contract_rows(hidden_normed, grad_gate_low)
    grad_up = contract_rows(hidden_normed, grad_up_low)
    grad_normed_ffn = lax.psum(
        (contract_cols(grad_gate_low, full_gate) + contract_cols(grad_up_low, full_up)).astype(
            jnp.bfloat16
        ),
        "tp",
    ).astype(jnp.float32)
    grad_ffn_gain = jnp.sum(grad_normed_ffn * hidden * second_inv, axis=0)
    grad_hidden = pulled.astype(jnp.float32) + norm_back(
        hidden, second_inv, gain_ffn.astype(jnp.float32), grad_normed_ffn
    )
    grad_hidden_low = grad_hidden.astype(jnp.bfloat16)
    gain_attn, full_query, full_key, full_value, full_output, gain_query, gain_key = (
        lax.all_gather(attn_gain, ("fsdp", "ctx"), axis=0, tiled=True),
        lax.all_gather(w_query, ("fsdp", "ctx"), axis=0, tiled=True),
        lax.all_gather(w_key, ("fsdp", "ctx"), axis=0, tiled=True),
        lax.all_gather(w_value, ("fsdp", "ctx"), axis=0, tiled=True),
        lax.all_gather(w_output, ("fsdp", "ctx"), axis=1, tiled=True),
        lax.all_gather(query_gain, ("fsdp", "ctx"), axis=0, tiled=True),
        lax.all_gather(key_gain, ("fsdp", "ctx"), axis=0, tiled=True),
    )
    grad_output = contract_rows(mixed_low, grad_hidden_low)
    grad_mixed = (
        contract_cols(grad_hidden_low, full_output)
        .astype(jnp.bfloat16)
        .reshape(rows, key_heads, groups, HEAD)
    )
    delta = jnp.einsum("qkge,qkge->kgq", grad_mixed.astype(jnp.float32), mixed)

    def grad_step(accum, block_id):

        def grad_work(current):
            key_block, value_block, allowed, scores = block_scores(block_id)
            probs = jnp.where(allowed, jnp.exp(scores - log_total[..., None]), 0.0)
            grad_value_block = jnp.einsum(
                "kgqt,qkge->tke",
                probs.astype(jnp.bfloat16),
                grad_mixed,
                preferred_element_type=jnp.float32,
            )
            grad_probs = jnp.einsum(
                "qkge,tke->kgqt", grad_mixed, value_block, preferred_element_type=jnp.float32
            )
            grad_scores = (probs * (grad_probs - delta[..., None])).astype(jnp.bfloat16)
            updated = (
                current
                + jnp.einsum(
                    "kgqt,tke->qkge", grad_scores, key_block, preferred_element_type=jnp.float32
                )
                * scale
            )
            grad_key_block = (
                jnp.einsum(
                    "kgqt,qkge->tke", grad_scores, query_rot, preferred_element_type=jnp.float32
                )
                * scale
            )
            terms = jnp.concatenate(
                [
                    grad_key_block.reshape(block, kv_width),
                    grad_value_block.reshape(block, kv_width),
                ],
                axis=1,
            )
            return (updated, terms)

        def skipped(current):
            return (current, jnp.zeros((block, 2 * kv_width), jnp.float32))

        return lax.cond(block_id * block <= last_row, grad_work, skipped, accum)

    grad_query_rot, key_terms = lax.scan(
        grad_step, jnp.zeros((rows, key_heads, groups, HEAD), jnp.float32), block_ids
    )
    own_terms = lax.psum_scatter(
        key_terms.reshape(length, 2 * kv_width).astype(jnp.bfloat16),
        "ctx",
        scatter_dimension=0,
        tiled=True,
    ).astype(jnp.float32)
    grad_key_rot = own_terms[:, :kv_width].reshape(rows, key_heads, HEAD)
    grad_value_low = own_terms[:, kv_width:].astype(jnp.bfloat16)
    grad_query_norm = unrotate(grad_query_rot.reshape(rows, query_heads, HEAD), cosine, sine)
    grad_key_norm = unrotate(grad_key_rot, cosine, sine)
    query_gain_part = jnp.sum(grad_query_norm * queries * query_inv, axis=(0, 1))
    key_gain_part = jnp.sum(grad_key_norm * keys * key_inv, axis=(0, 1))
    grad_query_low = (
        norm_back(queries, query_inv, gain_query.astype(jnp.float32), grad_query_norm)
        .astype(jnp.bfloat16)
        .reshape(rows, query_heads * HEAD)
    )
    grad_key_low = (
        norm_back(keys, key_inv, gain_key.astype(jnp.float32), grad_key_norm)
        .astype(jnp.bfloat16)
        .reshape(rows, kv_width)
    )
    grad_query = contract_rows(normed, grad_query_low)
    grad_key = contract_rows(normed, grad_key_low)
    grad_value = contract_rows(normed, grad_value_low)
    normed_terms = (
        contract_cols(grad_query_low, full_query)
        + contract_cols(grad_key_low, full_key)
        + contract_cols(grad_value_low, full_value)
    )
    grad_normed, grad_qgain, grad_kgain = (
        lax.psum(normed_terms.astype(jnp.bfloat16), "tp").astype(jnp.float32),
        lax.psum(query_gain_part.astype(jnp.bfloat16), "tp").astype(jnp.float32),
        lax.psum(key_gain_part.astype(jnp.bfloat16), "tp").astype(jnp.float32),
    )
    grad_attn_gain = jnp.sum(grad_normed * tokens * first_inv, axis=0)
    grad_inputs = grad_hidden + norm_back(
        tokens, first_inv, gain_attn.astype(jnp.float32), grad_normed
    )
    attn_grads = (
        lax.psum_scatter(grad_attn_gain, ("fsdp", "ctx"), scatter_dimension=0, tiled=True),
        lax.psum_scatter(grad_query, ("fsdp", "ctx"), scatter_dimension=0, tiled=True),
        lax.psum_scatter(grad_key, ("fsdp", "ctx"), scatter_dimension=0, tiled=True),
        lax.psum_scatter(grad_value, ("fsdp", "ctx"), scatter_dimension=0, tiled=True),
        lax.psum_scatter(grad_output, ("fsdp", "ctx"), scatter_dimension=1, tiled=True),
        lax.psum_scatter(grad_qgain, ("fsdp", "ctx"), scatter_dimension=0, tiled=True),
        lax.psum_scatter(grad_kgain, ("fsdp", "ctx"), scatter_dimension=0, tiled=True),
    )
    ffn_grads = (
        lax.psum_scatter(grad_ffn_gain, ("fsdp", "ctx"), scatter_dimension=0, tiled=True),
        lax.psum_scatter(grad_gate, ("fsdp", "ctx"), scatter_dimension=0, tiled=True),
        lax.psum_scatter(grad_up, ("fsdp", "ctx"), scatter_dimension=0, tiled=True),
        lax.psum_scatter(grad_down, ("fsdp", "ctx"), scatter_dimension=1, tiled=True),
    )
    return (
        result,
        grad_inputs[None],
        attn_grads[0],
        attn_grads[1],
        attn_grads[2],
        attn_grads[3],
        attn_grads[4],
        attn_grads[5],
        attn_grads[6],
        ffn_grads[0],
        ffn_grads[1],
        ffn_grads[2],
        ffn_grads[3],
    )


def solution(mesh):
    placed = (
        P("fsdp", "ctx", None),
        P("fsdp", "ctx", None),
        P("fsdp", None),
        P(("fsdp", "ctx")),
        P(("fsdp", "ctx"), "tp"),
        P(("fsdp", "ctx"), "tp"),
        P(("fsdp", "ctx"), "tp"),
        P("tp", ("fsdp", "ctx")),
        P(("fsdp", "ctx")),
        P(("fsdp", "ctx")),
        P(("fsdp", "ctx")),
        P(("fsdp", "ctx"), "tp"),
        P(("fsdp", "ctx"), "tp"),
        P("tp", ("fsdp", "ctx")),
    )
    return jax.shard_map(
        body,
        mesh=mesh,
        in_specs=placed,
        out_specs=(
            P("fsdp", "ctx", None),
            P("fsdp", "ctx", None),
            P(("fsdp", "ctx")),
            P(("fsdp", "ctx"), "tp"),
            P(("fsdp", "ctx"), "tp"),
            P(("fsdp", "ctx"), "tp"),
            P("tp", ("fsdp", "ctx")),
            P(("fsdp", "ctx")),
            P(("fsdp", "ctx")),
            P(("fsdp", "ctx")),
            P(("fsdp", "ctx"), "tp"),
            P(("fsdp", "ctx"), "tp"),
            P("tp", ("fsdp", "ctx")),
        ),
        check_vma=False,
    )
```

profile of v0, /device:TPU:0, one launch (start us, length us, event | category | flops | bytes accessed | tf_op | source)
XLA Modules:
  0.0 1640.3 jit_solution(13667922213039344715)
XLA Ops:
  8.7 46.7 %all_gather.51 = bf16[1536,256]{1,0:T(8,128)(2,1)S(1)} all-gather(bf16[96,256]{1,0:T(8,128)(2,1)} %param.32), channel_id=1, replica_groups=mesh['fsdp'=4,'ctx'=4,'tp'=2] {'fsdp','ctx'}, dimensions={0}, use_global_device_ids=true | all-gather | bytes 835584 | tf_op jit(solution)/shard_map/all_gather | solution.py:92
  61.4 33.3 %all-reduce.9 = (bf16[1536]{0:T(1024)(128)(2,1)S(1)}, bf16[64]{0:T(256)(128)(2,1)S(1)}, bf16[64]{0:T(256)(128)(2,1)S(1)}, bf16[1536]{0:T(1024)(128)(2,1)S(1)}) all-reduce(bf16[1536]{0:T(1024)(128)(2,1)S(1)} %dynamic-update-slice, bf16[64]{0:T(256)(128)(2,1)S(1)} %dynamic-update-slice.1, ...), channel_id=1, replica_groups=mesh['fsdp'=4,'ctx'=4,'tp'=2] {'fsdp','ctx'}, use_global_device_ids=true, to_apply=%add | all-reduce | flops 3200 | bytes 12800
  96.0 16.3 all_gather.52
  113.3 36.3 %all_gather.53 = bf16[1536,256]{1,0:T(8,128)(2,1)S(1)} all-gather(bf16[96,256]{1,0:T(8,128)(2,1)S(1)} %copy-done.43), channel_id=1, replica_groups=mesh['fsdp'=4,'ctx'=4,'tp'=2] {'fsdp','ctx'}, dimensions={0}, use_global_device_ids=true | all-gather | bytes 835584 | tf_op jit(solution)/shard_map/all_gather | solution.py:91
  153.7 15.3 all_gather.55
  169.0 4.3 copy.53
  173.2 2.6 multiply_reduce_fusion.3
  177.2 10.4 while.46
  179.7 5.3 conditional.12
  188.2 11.5 while.47
  190.8 6.4 conditional.13
  194.6 2.5 fusion.27
  199.8 3.7 convolution_convert_fusion.1
  205.6 43.2 %all-reduce.16.cloned.1.call-done = bf16[256,1536]{1,0:T(8,128)(2,1)} async-done(((bf16[256,1536]{1,0:T(8,128)(2,1)}), bf16[256,1536]{1,0:T(8,128)(2,1)}) %all-reduce.16.cloned.1.call-update) | async-done | bytes 786448 | tf_op jit(solution)/shard_map/psum | solution.py:200
  250.7 89.3 %all-gather.10.cloned.1.call-done = bf16[1536,3456]{1,0:T(8,128)(2,1)} async-done(((bf16[96,3456]{1,0:T(8,128)(2,1)}), bf16[1536,3456]{1,0:T(8,128)(2,1)}) %all-gather.10.cloned.1.call-update) | async-done | bytes 10616848 | tf_op jit(solution)/shard_map/all_gather | solution.py:99
  339.9 8.8 fusion.110
  348.7 80.5 %all-gather.12.cloned.1.call-done = bf16[1536,3456]{1,0:T(8,128)(2,1)} async-done(((bf16[96,3456]{1,0:T(8,128)(2,1)}), bf16[1536,3456]{1,0:T(8,128)(2,1)}) %all-gather.12.cloned.1.call-update) | async-done | bytes 10616848 | tf_op jit(solution)/shard_map/all_gather | solution.py:100
  429.2 8.8 fusion.111
  438.0 80.5 %all-gather.14.cloned.1.call-done = bf16[3456,1536]{0,1:T(8,128)(2,1)} async-done(((bf16[3456,96]{0,1:T(8,128)(2,1)}), bf16[3456,1536]{0,1:T(8,128)(2,1)}) %all-gather.14.cloned.1.call-update) | async-done | bytes 10616848 | tf_op jit(solution)/shard_map/all_gather | solution.py:101
  518.5 11.5 multiply_convert_fusion
  530.0 7.1 fusion.112
  537.2 3.9 fusion.47
  541.6 32.2 %all-reduce.18.cloned.1.call-done = bf16[256,1536]{1,0:T(8,128)(2,1)} async-done(((bf16[256,1536]{1,0:T(8,128)(2,1)}), bf16[256,1536]{1,0:T(8,128)(2,1)}) %all-reduce.18.cloned.1.call-update) | async-done | bytes 786448 | tf_op jit(solution)/shard_map/psum | solution.py:231
  573.8 2.4 fusion.64
  576.2 3.9 convolution_convert_fusion.2
  582.1 18.6 %while.48 = (s32[]{:T(128)}, f32[256,4,3,64]{0,3,2,1:T(8,128)S(1)}, bf16[2,512,512]{2,1,0:T(8,128)(2,1)}, s32[2]{0:T(128)S(1)}, s32[]{:T(128)}, /*index=5*/bf16[...) while((s32[]{:T(128)}, f32[256,4,3,64]{0,3,2,1:T(8,128)S(1)}, ...), condition=%wide.region_21.22_spmd.clone.clone, body=%wide.region_18.21_spmd.clone.clone.sunk | while | flops 1024463616 | bytes 38982188 | solution.py:301
  584.7 11.3 conditional.14
  589.3 2.8 fusion.33
  592.8 2.1 fusion.37
  601.0 8.5 convolution_convert_fusion
  613.2 26.2 %reduce-scatter.9.cloned.1.call-done = bf16[256,512]{1,0:T(8,128)(2,1)} async-done(((bf16[1024,512]{1,0:T(8,128)(2,1)}), bf16[256,512]{1,0:T(8,128)(2,1)}) %reduce-scatter.9.cloned.1.call-update) | async-done | bytes 262160 | tf_op jit(solution)/shard_map/reduce_scatter | solution.py:304
  641.0 1.8 copy.58
  647.8 1.7 fusion.84
  649.6 1.7 fusion.91
  651.3 3.1 fusion.86
  656.0 4.5 fusion.88
  661.6 10.3 fusion.114
  672.0 10.7 fusion.115
  683.8 10.3 fusion.76
  695.2 4.9 all-reduce.10
  701.8 59.8 %all-reduce.8 = (f32[1536]{0:T(1024)S(1)}, f32[64]{0:T(128)S(1)}, f32[64]{0:T(128)S(1)}, f32[1536]{0:T(1024)S(1)}) all-reduce(f32[1536]{0:T(1024)S(1)} %get-tuple-element.592, bf16[64]{0:T(256)(128)(2,1)S(1)} %get-tuple-element.680, ...), channel_id=3, replica_groups=mesh['fsdp'=4,'ctx'=4,'tp'=2] {'fsdp','ctx'}, use_global_device_ids=true, to_apply=%region_28.29.clone | all-reduce | flops 3200 | bytes 25344
  763.9 3.9 fusion.59
  767.9 57.3 %reduce-scatter.15.cloned.1.call-done = f32[96,256]{1,0:T(8,128)} async-done(((f32[1536,256]{1,0:T(8,128)}), f32[96,256]{1,0:T(8,128)}) %reduce-scatter.15.cloned.1.call-update) | async-done | bytes 98320 | tf_op jit(solution)/shard_map/reduce_scatter | solution.py:347
  825.2 78.9 %reduce-scatter.11.cloned.1.call-done = f32[96,768]{1,0:T(8,128)} async-done(((f32[1536,768]{1,0:T(8,128)}), f32[96,768]{1,0:T(8,128)}) %reduce-scatter.11.cloned.1.call-update) | async-done | bytes 294928 | tf_op jit(solution)/shard_map/reduce_scatter | solution.py:345
  904.1 79.6 %reduce-scatter.17.cloned.1.call-done = f32[768,96]{0,1:T(8,128)} async-done(((f32[768,1536]{0,1:T(8,128)}), f32[768,96]{0,1:T(8,128)}) %reduce-scatter.17.cloned.1.call-update) | async-done | bytes 294928 | tf_op jit(solution)/shard_map/reduce_scatter | solution.py:348
  983.6 216.4 %reduce-scatter.19.cloned.1.call-done = f32[96,3456]{1,0:T(8,128)} async-done(((f32[1536,3456]{1,0:T(8,128)}), f32[96,3456]{1,0:T(8,128)}) %reduce-scatter.19.cloned.1.call-update) | async-done | bytes 1327120 | tf_op jit(solution)/shard_map/reduce_scatter | solution.py:354
  1200.0 217.1 %reduce-scatter.21.cloned.1.call-done = f32[96,3456]{1,0:T(8,128)} async-done(((f32[1536,3456]{1,0:T(8,128)}), f32[96,3456]{1,0:T(8,128)}) %reduce-scatter.21.cloned.1.call-update) | async-done | bytes 1327120 | tf_op jit(solution)/shard_map/reduce_scatter | solution.py:355
  1417.1 216.4 %reduce-scatter.23.cloned.1.call-done = f32[3456,96]{0,1:T(8,128)} async-done(((f32[3456,1536]{0,1:T(8,128)}), f32[3456,96]{0,1:T(8,128)}) %reduce-scatter.23.cloned.1.call-update) | async-done | bytes 1327120 | tf_op jit(solution)/shard_map/reduce_scatter | solution.py:356
  (284 shorter events, 65.9 us)
Async XLA Ops:
  7.2 87.5 %copy-start = (bf16[1,256,1536]{2,1,0:T(8,128)(2,1)S(1)}, bf16[1,256,1536]{2,1,0:T(8,128)(2,1)}, u32[]{:S(2)}) copy-start(bf16[1,256,1536]{2,1,0:T(8,128)(2,1)} %param.26) | copy-start | bytes 2359300
  7.2 161.8 %all-gather.6.cloned.1.call-start = ((), (), s32[]{:S(2)}) async-start(), calls=%async_computation.8 | async-start | bytes 2506752 | tf_op jit(solution)/shard_map/all_gather | solution.py:90
  7.9 191.9 %all-gather.8.cloned.1.call-start = ((), (), s32[]{:S(2)}) async-start(), calls=%async_computation.9 | async-start | bytes 2506752 | tf_op jit(solution)/shard_map/all_gather | solution.py:93
  8.7 240.1 %all-reduce.16.cloned.1.call-start = ((), (), s32[]{:S(2)}) async-start(), calls=%async_computation.10 | async-start | bytes 1572864 | tf_op jit(solution)/shard_map/psum | solution.py:200
  55.4 56.9 %copy-start.18 = (bf16[1536,256]{1,0:T(8,128)(2,1)}, bf16[1536,256]{1,0:T(8,128)(2,1)S(1)}, u32[]{:S(2)}) copy-start(bf16[1536,256]{1,0:T(8,128)(2,1)S(1)} %all_gather.51) | copy-start | bytes 2359300
  94.7 78.5 %copy-start.32 = (f32[1536]{0:T(1024)}, f32[1536]{0:T(1024)S(1)}, u32[]{:S(2)}) copy-start(f32[1536]{0:T(1024)S(1)} %convert_element_type.205) | copy-start | bytes 18436
  95.6 77.7 %copy-start.40 = (f32[256]{0:T(256)}, f32[256]{0:T(256)S(1)}, u32[]{:S(2)}) copy-start(f32[256]{0:T(256)S(1)} %get-tuple-element.728) | copy-start | bytes 3076
  95.6 17.8 %copy-start.43 = (bf16[96,256]{1,0:T(8,128)(2,1)S(1)}, bf16[96,256]{1,0:T(8,128)(2,1)}, u32[]{:S(2)}) copy-start(bf16[96,256]{1,0:T(8,128)(2,1)} %param.31) | copy-start | bytes 147460
  112.3 37.6 %copy-start.34 = (s32[1,2]{1,0:T(1,128)S(1)}, s32[1,2]{1,0:T(1,128)}, u32[]{:S(2)}) copy-start(s32[1,2]{1,0:T(1,128)} %param.28) | copy-start | bytes 28
  149.9 26.6 %copy-start.52 = (f32[64]{0:T(128)}, f32[64]{0:T(128)S(1)}, u32[]{:S(2)}) copy-start(f32[64]{0:T(128)S(1)} %convert_element_type.216) | copy-start | bytes 772
  153.2 23.5 %copy-start.27 = (f32[256,32]{0,1:T(8,128)}, f32[256,32]{0,1:T(8,128)S(1)}, u32[]{:S(2)}) copy-start(f32[256,32]{0,1:T(8,128)S(1)} %get-tuple-element.725) | copy-start | bytes 98308
  153.2 23.5 %copy-start.29 = (f32[256,32]{0,1:T(8,128)}, f32[256,32]{0,1:T(8,128)S(1)}, u32[]{:S(2)}) copy-start(f32[256,32]{0,1:T(8,128)S(1)} %get-tuple-element.726) | copy-start | bytes 98308
  199.7 3.8 copy-start.8
  203.6 136.4 %all-gather.10.cloned.1.call-start = ((), (), s32[]{:S(2)}) async-start(), calls=%async_computation.11 | async-start | bytes 11280384 | tf_op jit(solution)/shard_map/all_gather | solution.py:99
  204.1 225.1 %all-gather.12.cloned.1.call-start = ((), (), s32[]{:S(2)}) async-start(), calls=%async_computation.12 | async-start | bytes 11280384 | tf_op jit(solution)/shard_map/all_gather | solution.py:100
  204.7 313.8 %all-gather.14.cloned.1.call-start = ((), (), s32[]{:S(2)}) async-start(), calls=%async_computation.13 | async-start | bytes 11280384 | tf_op jit(solution)/shard_map/all_gather | solution.py:101
  205.3 368.5 %all-reduce.18.cloned.1.call-start = ((), (), s32[]{:S(2)}) async-start(), calls=%async_computation.14 | async-start | bytes 1572864 | tf_op jit(solution)/shard_map/psum | solution.py:231
  250.3 325.8 %copy-start.45 = (f32[256]{0:T(256)}, f32[256]{0:T(256)S(1)}, u32[]{:S(2)}) copy-start(f32[256]{0:T(256)S(1)} %get-tuple-element.730) | copy-start | bytes 3076
  250.3 325.8 %copy-start.48 = (f32[256]{0:T(256)}, f32[256]{0:T(256)S(1)}, u32[]{:S(2)}) copy-start(f32[256]{0:T(256)S(1)} %get-tuple-element.729) | copy-start | bytes 3076
  250.6 178.6 %copy-start.3 = (bf16[256,1536]{1,0:T(8,128)(2,1)}, bf16[256,1536]{1,0:T(8,128)(2,1)S(1)}, u32[]{:S(2)}) copy-start(bf16[256,1536]{1,0:T(8,128)(2,1)S(1)} %multiply_convert_fusion.3) | copy-start | bytes 2359300
  518.5 18.6 %slice-start = ((s8[10616832]{0:T(1024)(128)(4,1)}), s8[4194304]{0:T(1024)(128)(4,1)S(1)}, s32[]{:S(2)}) async-start(s8[10616832]{0:T(1024)(128)(4,1)} %bitcast.290), calls=%async_computation.24 | async-start | bytes 8388608
  518.5 18.7 %slice-start.1 = ((s8[10616832]{0:T(1024)(128)(4,1)}), s8[4194304]{0:T(1024)(128)(4,1)S(1)}, s32[]{:S(2)}) async-start(s8[10616832]{0:T(1024)(128)(4,1)} %bitcast.290), calls=%async_computation.25 | async-start | bytes 8388608
  530.0 7.1 copy-start.23
  530.0 7.1 copy-start.22
  530.0 7.2 slice-start.2
  541.2 98.2 %reduce-scatter.9.cloned.1.call-start = ((), (), s32[]{:S(2)}) async-start(), calls=%async_computation.15 | async-start | bytes 1310720 | tf_op jit(solution)/shard_map/reduce_scatter | solution.py:304
  576.2 4.0 copy-start.50
  576.2 5.1 copy-start.9
  600.7 99.4 %all-reduce.20.cloned.1.call-start = ((), (), s32[]{:S(2)}) async-start(), calls=%async_computation.23 | async-start | bytes 3145728 | tf_op jit(solution)/shard_map/psum | solution.py:212
  601.0 8.5 copy-start.28
  601.0 8.5 copy-start.30
  601.0 8.6 copy-start.36
  601.0 8.6 copy-start.53
  612.3 31.4 %copy-start.21 = (f32[256,4,64]{0,2,1:T(8,128)S(1)}, f32[256,4,64]{0,2,1:T(8,128)}, u32[]{:S(2)}) copy-start(f32[256,4,64]{0,2,1:T(8,128)} %copy-done.20) | copy-start | bytes 786436
  612.3 31.5 %copy-start.38 = (f32[256,4]{0,1:T(4,128)S(1)}, f32[256,4]{0,1:T(4,128)}, u32[]{:S(2)}) copy-start(f32[256,4]{0,1:T(4,128)} %copy-done.37) | copy-start | bytes 12292
  612.3 31.5 %copy-start.55 = (f32[64]{0:T(128)S(1)}, f32[64]{0:T(128)}, u32[]{:S(2)}) copy-start(f32[64]{0:T(128)} %copy-done.54) | copy-start | bytes 772
  613.1 31.3 %copy-start.47 = (f32[256,4]{0,1:T(4,128)S(1)}, f32[256,4]{0,1:T(4,128)}, u32[]{:S(2)}) copy-start(f32[256,4]{0,1:T(4,128)} %get-tuple-element.723) | copy-start | bytes 12292
  613.2 32.1 %copy-start.13 = (bf16[1536,256]{1,0:T(8,128)(2,1)S(1)}, bf16[1536,256]{1,0:T(8,128)(2,1)}, u32[]{:S(2)}) copy-start(bf16[1536,256]{1,0:T(8,128)(2,1)} %copy-done.12) | copy-start | bytes 2359300
  647.7 120.2 %reduce-scatter.13.cloned.1.call-start = ((), (), s32[]{:S(2)}) async-start(), calls=%async_computation.17 | async-start | bytes 1671168 | tf_op jit(solution)/shard_map/reduce_scatter | solution.py:346
  649.5 175.7 %reduce-scatter.15.cloned.1.call-start = ((), (), s32[]{:S(2)}) async-start(), calls=%async_computation.18 | async-start | bytes 1671168 | tf_op jit(solution)/shard_map/reduce_scatter | solution.py:347
  651.3 252.8 %reduce-scatter.11.cloned.1.call-start = ((), (), s32[]{:S(2)}) async-start(), calls=%async_computation.16 | async-start | bytes 5013504 | tf_op jit(solution)/shard_map/reduce_scatter | solution.py:345
  654.4 329.2 %reduce-scatter.17.cloned.1.call-start = ((), (), s32[]{:S(2)}) async-start(), calls=%async_computation.19 | async-start | bytes 5013504 | tf_op jit(solution)/shard_map/reduce_scatter | solution.py:348
  660.5 539.5 %reduce-scatter.19.cloned.1.call-start = ((), (), s32[]{:S(2)}) async-start(), calls=%async_computation.20 | async-start | bytes 22560768 | tf_op jit(solution)/shard_map/reduce_scatter | solution.py:354
  672.0 745.1 %reduce-scatter.21.cloned.1.call-start = ((), (), s32[]{:S(2)}) async-start(), calls=%async_computation.21 | async-start | bytes 22560768 | tf_op jit(solution)/shard_map/reduce_scatter | solution.py:355
  682.7 950.8 %reduce-scatter.23.cloned.1.call-start = ((), (), s32[]{:S(2)}) async-start(), calls=%async_computation.22 | async-start | bytes 22560768 | tf_op jit(solution)/shard_map/reduce_scatter | solution.py:356
  694.1 6.1 copy-start.42
  694.1 7.7 copy-start.44
  694.1 69.9 %copy-start.56 = (f32[256]{0:T(256)S(1)}, f32[256]{0:T(256)}, u32[]{:S(2)}) copy-start(f32[256]{0:T(256)} %get-tuple-element.727) | copy-start | bytes 3076
  (34 other events, 54.7 us)
Sparse Core Ops, SparseCore 0:
  10.3 47.2 all-gather.5
  59.9 42.6 all-gather.7
  203.7 45.0 all-reduce.15
  251.2 88.6 all-gather.9
  342.3 86.8 all-gather.11
  431.6 86.8 all-gather.13
  541.3 32.4 all-reduce.17
  600.9 38.4 reduce-scatter.8
  647.9 50.3 all-reduce.19
  702.3 59.6 reduce-scatter.12
  766.7 58.4 reduce-scatter.14
  829.5 74.5 reduce-scatter.10
  909.0 74.5 reduce-scatter.16
  988.2 211.7 reduce-scatter.18
  1205.1 211.9 reduce-scatter.20
  1421.6 211.8 reduce-scatter.22
where the time goes:
time: 1650 us; the launch traced here: 1640 us
  waiting for transfers between devices  1220 us (74%)
  blocking collectives  213 us (13%)
  matrix products  116 us (7%)
  other arithmetic  33.5 us (2%)
  local copies, waits for them, and re-layouts  32.5 us (2%)
  between operations  17.4 us (1%)
    reduce_scatter x1, waiting for transfers between devices, body(): lax.psum_scatter(grad_up, ('fsdp', 'ctx'), scatter_dimension=0, tiled=True)  217 us
    reduce_scatter x1, waiting for transfers between devices, body(): lax.psum_scatter(grad_down, ('fsdp', 'ctx'), scatter_dimension=1, tiled=T...  216 us
    reduce_scatter x1, waiting for transfers between devices, body(): lax.psum_scatter(grad_gate, ('fsdp', 'ctx'), scatter_dimension=0, tiled=T...  216 us
    unnamed x2, blocking collectives  93.1 us
    all_gather x1, waiting for transfers between devices, body(): lax.all_gather(w_gate, ('fsdp', 'ctx'), axis=0, tiled=True)  89.3 us
    all_gather x1, waiting for transfers between devices, body(): lax.all_gather(w_up, ('fsdp', 'ctx'), axis=0, tiled=True)  80.5 us
    all_gather x1, waiting for transfers between devices, body(): lax.all_gather(w_down, ('fsdp', 'ctx'), axis=1, tiled=True)  80.5 us
    reduce_scatter x1, waiting for transfers between devices, body(): lax.psum_scatter(grad_output, ('fsdp', 'ctx'), scatter_dimension=1, tiled...  79.6 us
  transfers between devices with their start and end apart: 16, of which 12 were waited for; matrix products, arithmetic and copies ran while one was open for 7% of the time, Pallas kernels for 0%

commit v1 on v0

v1 whole, which is shorter than its diff:
```python
import jax
import jax.numpy as jnp
from jax import lax
from jax.sharding import PartitionSpec as P

HQ = 24
HK = 8
HEAD = 64


EPS = 1e-05
THETA = 1000000.0
NEG = -1e30
LINE = 4


def inverse_rms(values):
    return lax.rsqrt(jnp.mean(values * values, axis=-1, keepdims=True) + EPS)


def rotate(values, cosine, sine):
    half = values.shape[-1] // 2
    front = values[..., :half]
    back = values[..., half:]
    return jnp.concatenate([front * cosine - back * sine, back * cosine + front * sine], axis=-1)


def unrotate(grads, cosine, sine):
    half = grads.shape[-1] // 2
    front = grads[..., :half]
    back = grads[..., half:]
    return jnp.concatenate([front * cosine + back * sine, back * cosine - front * sine], axis=-1)


def norm_back(values, inverse, gain, grads):
    scaled = grads * gain
    return inverse * scaled - values * (inverse * inverse * inverse) * jnp.mean(
        scaled * values, axis=-1, keepdims=True
    )


def contract_rows(left, right):
    return lax.dot_general(
        left, right, (((0,), (0,)), ((), ())), preferred_element_type=jnp.float32
    )


def contract_cols(left, right):
    return lax.dot_general(
        left, right, (((1,), (1,)), ((), ())), preferred_element_type=jnp.float32
    )


def document(index, bounds):
    return (index >= bounds[0]).astype(jnp.int32) + (index >= bounds[1]).astype(jnp.int32)


def doc_position(index, bounds):
    begin = jnp.where(index >= bounds[1], bounds[1], jnp.where(index >= bounds[0], bounds[0], 0))
    return index - begin


def tables(where_in):
    freq = THETA ** (-(jnp.arange(HEAD // 2, dtype=jnp.float32) * 2.0 / HEAD))
    angle = where_in.astype(jnp.float32)[:, None] * freq[None, :]
    return (jnp.cos(angle)[:, None, :], jnp.sin(angle)[:, None, :])


def keep_state(current):
    return current


def pick(stack, index, axis=0):
    return lax.dynamic_index_in_dim(stack, index, axis, keepdims=False)


def place(stack, part, index, axis=0):
    return lax.dynamic_update_index_in_dim(stack, part, index, axis)


def flip(part, bit):
    size = lax.axis_size("fsdp")
    return lax.ppermute(part, "fsdp", [(i, i ^ bit) for i in range(size)])


def swap(part):
    return lax.ppermute(part, "tp", [(0, 1), (1, 0)])


def line_gather(part, both=True, axis=0):
    size = lax.axis_size("ctx")
    if size > LINE:
        return lax.all_gather(part, "ctx", axis=axis)
    me = lax.axis_index("ctx")
    rights = [part]
    lefts = [part]
    for step in range(1, size):
        rights.append(
            lax.ppermute(rights[-1], "ctx", [(i, i + 1) for i in range(step - 1, size - 1)])
        )
        if both:
            lefts.append(
                lax.ppermute(lefts[-1], "ctx", [(i, i - 1) for i in range(1, size - step + 1)])
            )
    shape = part.shape[:axis] + (size,) + part.shape[axis:]
    whole = place(jnp.zeros(shape, part.dtype), part, me, axis)
    for step in range(1, size):
        other = lefts[size - step] if both else jnp.zeros_like(part)
        block = jnp.where(me >= step, rights[step], other)
        whole = place(whole, block, lax.rem(me - step + size, size), axis)
    return whole


def line_scatter(take, both=True):
    size = lax.axis_size("ctx")
    me = lax.axis_index("ctx")
    low = jnp.bfloat16

    def term(index):
        return take(jnp.clip(index, 0, size - 1)).astype(jnp.float32)

    from_left = None
    from_right = None
    for step in range(1, size):
        ahead = size - step
        if both:
            send = term(me + ahead)
            if from_left is not None:
                send = send + from_left.astype(jnp.float32)
            from_left = lax.ppermute(
                send.astype(low), "ctx", [(i, i + 1) for i in range(0, size - ahead)]
            )
        send = term(me - ahead)
        if from_right is not None:
            send = send + from_right.astype(jnp.float32)
        from_right = lax.ppermute(
            send.astype(low), "ctx", [(i, i - 1) for i in range(ahead, size)]
        )
    total = term(me) + from_right.astype(jnp.float32)
    if both:
        total = total + from_left.astype(jnp.float32)
    return total


def group_gather(part):
    me = lax.axis_index("fsdp")
    across = flip(part, 2)
    beside = flip(part, 1)
    corner = flip(across, 1)
    whole = jnp.zeros((lax.axis_size("fsdp"),) + part.shape, part.dtype)
    whole = place(whole, part, me)
    whole = place(whole, across, me ^ 2)
    whole = place(whole, beside, me ^ 1)
    return place(whole, corner, me ^ 3)


def group_scatter(terms):
    me = lax.axis_index("fsdp")
    far = pick(terms, me ^ 2).astype(jnp.float32) + flip(pick(terms, me ^ 3), 1).astype(
        jnp.float32
    )
    near = pick(terms, me).astype(jnp.float32) + flip(pick(terms, me ^ 1), 1).astype(jnp.float32)
    return near + flip(far.astype(jnp.bfloat16), 2).astype(jnp.float32)


def group_trade(parts):
    me = lax.axis_index("fsdp")
    whole = place(jnp.zeros_like(parts), pick(parts, me), me)
    for bit in (1, 2, 3):
        whole = place(whole, flip(pick(parts, me ^ bit), bit), me ^ bit)
    return whole


def gather_all(part):
    return group_gather(line_gather(part))


def scatter_all(terms):
    size = lax.axis_size("ctx")
    parts = lax.axis_size("fsdp")
    low = jnp.bfloat16
    own = group_scatter(terms.reshape(parts, size, -1, terms.shape[-1])).astype(low)
    if size > LINE:
        return lax.psum_scatter(own, "ctx", scatter_dimension=0, tiled=False).astype(jnp.float32)
    return line_scatter(lambda index: pick(own, index))


def scatter_hidden(terms):
    size = lax.axis_size("ctx")
    parts = lax.axis_size("fsdp")
    width = terms.shape[-1]
    blocks = terms.reshape(parts, size, -1, width)
    if size > LINE:
        own = lax.psum_scatter(blocks, "ctx", scatter_dimension=1, tiled=False)
    else:
        own = line_scatter(lambda index: pick(blocks, index, 1)).astype(jnp.bfloat16)
    traded = group_trade(own)
    return jnp.concatenate([traded[i] for i in range(parts)], axis=-1).astype(jnp.float32)


def body(
    inputs,
    cotangent,
    doc_bounds,
    attn_gain,
    w_query,
    w_key,
    w_value,
    w_output,
    query_gain,
    key_gain,
    ffn_gain,
    w_gate,
    w_up,
    w_down,
):
    parts = lax.axis_size("fsdp")
    size = lax.axis_size("ctx")
    tensor = lax.axis_size("tp")
    me = lax.axis_index("ctx")
    low = jnp.bfloat16
    share = w_query.shape[0]
    model = share * parts * size
    query_heads = HQ // tensor
    key_heads = HK // tensor
    groups = HQ // HK
    kv_width = key_heads * HEAD
    small = query_gain.shape[0]

    gains = jnp.concatenate([attn_gain, ffn_gain, query_gain, key_gain])
    pad = 16
    gain_rows = jnp.zeros((pad, 2 * kv_width), low).at[0, : gains.shape[0]].set(gains)
    kv_block = jnp.concatenate(
        [jnp.concatenate([w_key, w_value], axis=1), gain_rows], axis=0
    )
    whole_kv = gather_all(kv_block)
    full_kv = whole_kv[:, :, :share].reshape(model, 2 * kv_width)
    all_gains = whole_kv[:, :, share].reshape(parts * size, 2 * kv_width).astype(jnp.float32)
    gain_attn = all_gains[:, :share].reshape(model)
    gain_ffn = all_gains[:, share : 2 * share].reshape(model)
    gain_query = all_gains[:, 2 * share : 2 * share + small].reshape(HEAD)
    gain_key = all_gains[:, 2 * share + small : 2 * share + 2 * small].reshape(HEAD)
    full_query = gather_all(w_query).reshape(model, query_heads * HEAD)
    full_output = gather_all(w_output.T).reshape(model, query_heads * HEAD)

    hidden_part = w_gate.shape[1] // parts
    stacked = jnp.stack([w_gate, w_up, w_down.T]).reshape(3, share, parts, hidden_part)
    traded = group_trade(stacked.transpose(2, 0, 1, 3))
    full_gate, full_up, full_down = (
        line_gather(traded[:, i], axis=1).reshape(model, hidden_part) for i in range(3)
    )
    pulled = cotangent[0]

    tokens = inputs[0].astype(jnp.float32)
    rows = tokens.shape[0]
    pulled_all = group_gather(pulled).reshape(parts * rows, model)
    length = rows * size
    first = me * rows
    last_row = first + rows - 1
    bounds = doc_bounds[0]
    row_index = first + jnp.arange(rows, dtype=jnp.int32)
    row_docs = document(row_index, bounds)
    cosine, sine = tables(doc_position(row_index, bounds))
    scale = HEAD ** (-0.5)
    first_inv = inverse_rms(tokens)
    normed = (tokens * first_inv * gain_attn).astype(low)
    keys_values = jnp.dot(normed, full_kv, preferred_element_type=jnp.float32)
    keys = keys_values[:, :kv_width].reshape(rows, key_heads, HEAD)
    values = keys_values[:, kv_width:].astype(low)
    key_inv = inverse_rms(keys)
    key_rot = rotate(keys * key_inv * gain_key, cosine, sine).astype(low).reshape(rows, kv_width)
    gathered = line_gather(jnp.concatenate([key_rot, values], axis=1), both=False)
    gathered = gathered.reshape(length, 2 * kv_width)
    all_keys = gathered[:, :kv_width]
    all_values = gathered[:, kv_width:]
    queries = jnp.dot(normed, full_query, preferred_element_type=jnp.float32).reshape(
        rows, query_heads, HEAD
    )
    query_inv = inverse_rms(queries)
    query_rot = (
        rotate(queries * query_inv * gain_query, cosine, sine)
        .astype(low)
        .reshape(rows, key_heads, groups, HEAD)
    )
    block = 512
    block_count = length // block
    block_ids = jnp.arange(block_count, dtype=jnp.int32)

    def block_scores(block_id):
        start = block_id * block
        key_block = lax.dynamic_slice_in_dim(all_keys, start, block, 0).reshape(
            block, key_heads, HEAD
        )
        value_block = lax.dynamic_slice_in_dim(all_values, start, block, 0).reshape(
            block, key_heads, HEAD
        )
        key_index = start + jnp.arange(block, dtype=jnp.int32)
        allowed = (key_index[None, :] <= row_index[:, None]) & (
            document(key_index, bounds)[None, :] == row_docs[:, None]
        )
        scores = (
            jnp.einsum("qkge,tke->kgqt", query_rot, key_block, preferred_element_type=jnp.float32)
            * scale
        )
        return (key_block, value_block, allowed, scores)

    def stats_step(state, block_id):

        def stats_work(current):
            top, total = current
            scores_all = block_scores(block_id)
            allowed = scores_all[2]
            scores = scores_all[3]
            new_top = jnp.maximum(top, jnp.max(jnp.where(allowed, scores, NEG), axis=-1))
            weights = jnp.where(allowed, jnp.exp(scores - new_top[..., None]), 0.0)
            return (new_top, total * jnp.exp(top - new_top) + jnp.sum(weights, axis=-1))

        return (lax.cond(block_id * block <= last_row, stats_work, keep_state, state), None)

    top_start = jnp.full((key_heads, groups, rows), NEG, jnp.float32)
    total_start = jnp.zeros((key_heads, groups, rows), jnp.float32)
    (top, total), _ = lax.scan(stats_step, (top_start, total_start), block_ids)
    log_total = top + jnp.log(total)

    def value_step(accum, block_id):

        def value_work(current):
            _, value_block, allowed, scores = block_scores(block_id)
            probs = jnp.where(allowed, jnp.exp(scores - log_total[..., None]), 0.0).astype(low)
            return current + jnp.einsum(
                "kgqt,tke->qkge", probs, value_block, preferred_element_type=jnp.float32
            )

        return (lax.cond(block_id * block <= last_row, value_work, keep_state, accum), None)

    mixed, _ = lax.scan(
        value_step, jnp.zeros((rows, key_heads, groups, HEAD), jnp.float32), block_ids
    )
    mixed_low = mixed.reshape(rows, query_heads * HEAD).astype(low)
    branch_part = contract_cols(mixed_low, full_output).astype(low)
    branch = branch_part.astype(jnp.float32) + swap(branch_part).astype(jnp.float32)
    hidden = tokens + branch
    second_inv = inverse_rms(hidden)
    hidden_normed = (hidden * second_inv * gain_ffn).astype(low)

    hidden_all = group_gather(hidden_normed).reshape(parts * rows, model)
    gate = jnp.dot(hidden_all, full_gate, preferred_element_type=jnp.float32)
    upward = jnp.dot(hidden_all, full_up, preferred_element_type=jnp.float32)
    sigma = jax.nn.sigmoid(gate)
    active = gate * sigma
    middle = (active * upward).astype(low)
    grad_down = scatter_hidden(contract_rows(pulled_all, middle).astype(low)).T
    grad_middle = jnp.dot(pulled_all, full_down, preferred_element_type=jnp.float32)
    grad_gate_low = (grad_middle * upward * sigma * (1.0 + gate * (1.0 - sigma))).astype(low)
    grad_up_low = (grad_middle * active).astype(low)
    normed_part = group_scatter(
        (contract_cols(grad_gate_low, full_gate) + contract_cols(grad_up_low, full_up))
        .astype(low)
        .reshape(parts, rows, model)
    ).astype(low)
    grad_normed_ffn = normed_part.astype(jnp.float32) + swap(normed_part).astype(jnp.float32)
    grad_gate = scatter_hidden(contract_rows(hidden_all, grad_gate_low).astype(low))
    grad_up = scatter_hidden(contract_rows(hidden_all, grad_up_low).astype(low))
    feed_part = group_scatter(
        contract_cols(middle, full_down).astype(low).reshape(parts, rows, model)
    ).astype(low)
    feed = feed_part.astype(jnp.float32) + swap(feed_part).astype(jnp.float32)
    result = (hidden + feed).astype(low)[None]

    ffn_gain_part = jnp.sum(grad_normed_ffn * hidden * second_inv, axis=0) * 0.5
    grad_hidden = pulled.astype(jnp.float32) + norm_back(
        hidden, second_inv, gain_ffn, grad_normed_ffn
    )
    grad_hidden_low = grad_hidden.astype(low)
    grad_output = scatter_all(contract_rows(grad_hidden_low, mixed_low).astype(low)).T
    grad_mixed = (
        jnp.dot(grad_hidden_low, full_output, preferred_element_type=jnp.float32)
        .astype(low)
        .reshape(rows, key_heads, groups, HEAD)
    )
    delta = jnp.einsum("qkge,qkge->kgq", grad_mixed.astype(jnp.float32), mixed)

    def grad_step(accum, block_id):

        def grad_work(current):
            key_block, value_block, allowed, scores = block_scores(block_id)
            probs = jnp.where(allowed, jnp.exp(scores - log_total[..., None]), 0.0)
            grad_value_block = jnp.einsum(
                "kgqt,qkge->tke",
                probs.astype(low),
                grad_mixed,
                preferred_element_type=jnp.float32,
            )
            grad_probs = jnp.einsum(
                "qkge,tke->kgqt", grad_mixed, value_block, preferred_element_type=jnp.float32
            )
            grad_scores = (probs * (grad_probs - delta[..., None])).astype(low)
            updated = (
                current
                + jnp.einsum(
                    "kgqt,tke->qkge", grad_scores, key_block, preferred_element_type=jnp.float32
                )
                * scale
            )
            grad_key_block = (
                jnp.einsum(
                    "kgqt,qkge->tke", grad_scores, query_rot, preferred_element_type=jnp.float32
                )
                * scale
            )
            terms = jnp.concatenate(
                [
                    grad_key_block.reshape(block, kv_width),
                    grad_value_block.reshape(block, kv_width),
                ],
                axis=1,
            )
            return (updated, terms)

        def skipped(current):
            return (current, jnp.zeros((block, 2 * kv_width), jnp.float32))

        return lax.cond(block_id * block <= last_row, grad_work, skipped, accum)

    grad_query_rot, key_terms = lax.scan(
        grad_step, jnp.zeros((rows, key_heads, groups, HEAD), jnp.float32), block_ids
    )
    key_terms = key_terms.reshape(size, rows, 2 * kv_width).astype(low)
    if size > LINE:
        own_terms = lax.psum_scatter(key_terms, "ctx", scatter_dimension=0, tiled=False).astype(
            jnp.float32
        )
    else:
        own_terms = line_scatter(lambda index: pick(key_terms, index), both=False)
    grad_query_norm = unrotate(grad_query_rot.reshape(rows, query_heads, HEAD), cosine, sine)
    query_gain_part = jnp.sum(grad_query_norm * queries * query_inv, axis=(0, 1))
    grad_query_low = (
        norm_back(queries, query_inv, gain_query, grad_query_norm)
        .astype(low)
        .reshape(rows, query_heads * HEAD)
    )
    grad_query = scatter_all(contract_rows(normed, grad_query_low).astype(low))

    grad_key_rot = own_terms[:, :kv_width].reshape(rows, key_heads, HEAD)
    grad_value_low = own_terms[:, kv_width:].astype(low)
    grad_key_norm = unrotate(grad_key_rot, cosine, sine)
    key_gain_part = jnp.sum(grad_key_norm * keys * key_inv, axis=(0, 1))
    grad_key_low = (
        norm_back(keys, key_inv, gain_key, grad_key_norm).astype(low).reshape(rows, kv_width)
    )
    grad_kv_low = jnp.concatenate([grad_key_low, grad_value_low], axis=1)
    normed_terms = contract_cols(grad_query_low, full_query) + contract_cols(grad_kv_low, full_kv)
    normed_low = normed_terms.astype(low)
    grad_normed = normed_low.astype(jnp.float32) + swap(normed_low).astype(jnp.float32)
    attn_gain_part = jnp.sum(normed_terms * tokens * first_inv, axis=0)
    shards = parts * size
    gain_parts = jnp.concatenate(
        [
            attn_gain_part.reshape(shards, share),
            ffn_gain_part.reshape(shards, share),
            query_gain_part.reshape(shards, small),
            key_gain_part.reshape(shards, small),
        ],
        axis=1,
    ).astype(low)
    width = gain_parts.shape[1]
    gain_block = jnp.zeros((shards, pad, 2 * kv_width), low).at[:, 0, :width].set(gain_parts)
    kv_terms = contract_rows(normed, grad_kv_low).astype(low).reshape(shards, share, 2 * kv_width)
    own_kv = scatter_all(
        jnp.concatenate([kv_terms, gain_block], axis=1).reshape(
            shards * (share + pad), 2 * kv_width
        )
    )
    grad_key = own_kv[:share, :kv_width]
    grad_value = own_kv[:share, kv_width:]
    own_gains = own_kv[share, :width].astype(low)
    grad_gains = own_gains.astype(jnp.float32) + swap(own_gains).astype(jnp.float32)
    grad_inputs = grad_hidden + norm_back(tokens, first_inv, gain_attn, grad_normed)
    return (
        result,
        grad_inputs[None],
        grad_gains[:share],
        grad_query,
        grad_key,
        grad_value,
        grad_output,
        grad_gains[2 * share : 2 * share + small],
        grad_gains[2 * share + small :],
        grad_gains[share : 2 * share],
        grad_gate,
        grad_up,
        grad_down,
    )


def solution(mesh):
    vector = P(("fsdp", "ctx"))
    columns = P(("fsdp", "ctx"), "tp")
    tall = P("tp", ("fsdp", "ctx"))
    act = P("fsdp", "ctx", None)
    return jax.shard_map(
        body,
        mesh=mesh,
        in_specs=(
            act,
            act,
            P("fsdp", None),
            vector,
            columns,
            columns,
            columns,
            tall,
            vector,
            vector,
            vector,
            columns,
            columns,
            tall,
        ),
        out_specs=(
            act,
            act,
            vector,
            columns,
            columns,
            columns,
            tall,
            vector,
            vector,
            vector,
            columns,
            columns,
            tall,
        ),
        check_vma=False,
    )
```

time: 1650 us -> 823 us (0.50)
  waiting for transfers between devices: 1220 us -> 161 us
  starting transfers between devices: 1.65 us -> 329 us
  blocking collectives: 213 us -> 0 us
  local copies, waits for them, and re-layouts: 32.5 us -> 137 us
  other arithmetic: 33.5 us -> 94.3 us
  matrix products: 116 us -> 78.2 us
    reduce_scatter x8 -> x0, waiting for transfers between devices: 892 us -> none  [the longest x1 217 us: body(): lax.psum_scatter(grad_up, ('fsdp', 'ctx'), scatter_dimension=0, tiled=True)]
    ppermute x0 -> x125, starting transfers between devices: none -> 329 us  [the longest x18 112 us: line_scatter(): lax.ppermute(send.astype(low), 'ctx', [(i, i + 1) for i in range(0, size...]
    all_gather x5 -> x0, waiting for transfers between devices: 250 us -> none  [the longest x1 89.3 us: body(): lax.all_gather(w_gate, ('fsdp', 'ctx'), axis=0, tiled=True)]
    ppermute x0 -> x125, waiting for transfers between devices: none -> 161 us  [the longest x42 73.2 us: flip(): return lax.ppermute(part, 'fsdp', [(i, i ^ bit) for i in range(size)])]
    all_gather x4 -> x0, blocking collectives: 115 us -> none  [the longest x1 46.7 us: body(): lax.all_gather(w_value, ('fsdp', 'ctx'), axis=0, tiled=True)]
    unnamed x2 -> x0, blocking collectives: 93.1 us -> none
    psum x3 -> x0, waiting for transfers between devices: 75.4 us -> none  [the longest x1 43.2 us: body(): lax.psum(jnp.dot(mixed_low, full_output, preferred_element_type=jnp.float...]
    convert_element_type x8 -> x38, other arithmetic: 1.33 us -> 36 us  [the longest x20 17.4 us: line_scatter(): send.astype(low)]
  transfers between devices with their start and end apart: 16 -> 125, of which waited for: 12 -> 29; matrix products, arithmetic and copies ran while one was open for 7% -> 32% of each run, Pallas kernels for 0% -> 0%
where the time goes in v1:
time: 823 us; the launch traced here: 810 us
  starting transfers between devices  329 us (40%)
  waiting for transfers between devices  161 us (20%)
  local copies, waits for them, and re-layouts  137 us (17%)
  other arithmetic  94.3 us (11%)
  matrix products  78.2 us (10%)
    ppermute x18, starting transfers between devices, line_scatter(): lax.ppermute(send.astype(low), 'ctx', [(i, i + 1) for i in range(0, size...  112 us
    ppermute x21, starting transfers between devices, line_gather(): lax.ppermute(rights[-1], 'ctx', [(i, i + 1) for i in range(step - 1, size...  80.8 us
    ppermute x42, waiting for transfers between devices, flip(): return lax.ppermute(part, 'fsdp', [(i, i ^ bit) for i in range(size)])  73.2 us
    ppermute x21, starting transfers between devices, line_scatter(): lax.ppermute(send.astype(low), 'ctx', [(i, i - 1) for i in range(ahead, s...  52.6 us
    ppermute x42, starting transfers between devices, flip(): return lax.ppermute(part, 'fsdp', [(i, i ^ bit) for i in range(size)])  51.6 us
    ppermute x18, waiting for transfers between devices, line_gather(): lax.ppermute(lefts[-1], 'ctx', [(i, i - 1) for i in range(1, size - step...  50.4 us
    ppermute x18, waiting for transfers between devices, line_scatter(): lax.ppermute(send.astype(low), 'ctx', [(i, i + 1) for i in range(0, size...  30.5 us
    dynamic_update_slice x38, local copies, waits for them, and re-layouts, place(): return lax.dynamic_update_index_in_dim(stack, part, index, axis)  28.4 us
  transfers between devices with their start and end apart: 125, of which 29 were waited for; matrix products, arithmetic and copies ran while one was open for 32% of the time, Pallas kernels for 0%

profile of v1, /device:TPU:0, one launch (start us, length us, event | category | flops | bytes accessed | tf_op | source)
XLA Modules:
  0.0 810.2 jit_solution(5326141259311642352)
XLA Ops:
  1.9 6.2 collective-permute-start.21
  11.7 5.2 collective-permute-start
  31.3 5.3 constant_dynamic-slice_fusion.5
  51.7 7.3 collective-permute-start.12
  61.1 6.9 collective-permute-start.59
  72.8 5.5 collective-permute-done.24
  101.4 10.1 %collective-permute-done.36 = bf16[3,96,864]{2,1,0:T(8,128)(2,1)S(1)} collective-permute-done((bf16[3,96,864]{2,1,0:T(8,128)(2,1)}, bf16[3,96,864]{2,1,0:T(8,128)(2,1)S(1)}, u32[]{:S(2)}, u32[]{:S(2)}) %collective-permute-start.36) | collective-permute-done | bytes 497696 | tf_op jit(solution)/shard_map/ppermute | solution.py:83
  111.4 9.3 %collective-permute-start.27 = (bf16[4,96,768]{2,1,0:T(8,128)(2,1)}, bf16[4,96,768]{2,1,0:T(8,128)(2,1)S(1)}, u32[]{:S(2)}, u32[]{:S(2)}) collective-permute-start(bf16[4,96,768]{2,1,0:T(8,128)(2,1)} %bitcast_dynamic-update-slice_fusion.48), channel_id=1, source_target_pairs={{0,16},{8,24},{16,0},{24,8},{1,17},{9,25},{17,1},{25,9},{2,18},{10... | collective-permute-start | bytes 1769480 | tf_op jit(solution)/shard_map/ppermute | solution.py:83
  136.9 6.2 collective-permute-start.37
  143.4 5.8 collective-permute-done.18
  167.3 5.7 collective-permute-start.9
  186.6 5.4 collective-permute-start.43
  205.7 6.7 dynamic_update_slice.216
  212.7 15.3 %collective-permute-start.49 = (bf16[4,96,864]{2,1,0:T(8,128)(2,1)}, bf16[4,96,864]{2,1,0:T(8,128)(2,1)}, u32[]{:S(2)}, u32[]{:S(2)}) collective-permute-start(bf16[4,96,864]{2,1,0:T(8,128)(2,1)} %get-tuple-element.703), channel_id=1, source_target_pairs={{0,2},{2,4},{4,6},{1,3},{3,5},{5,7},{8,10},{10,12},{12,14},{9,11},... | collective-permute-start | bytes 1990664 | tf_op jit(solution)/shard_map/ppermute | solution.py:99
  230.1 10.1 %while.48 = (s32[]{:T(128)}, f32[4,3,256]{2,1,0:T(4,128)S(1)}, f32[4,3,256]{2,1,0:T(4,128)S(1)}, s32[2]{0:T(128)S(1)}, s32[]{:T(128)}, /*index=5*/s32[2]{0:T(128...) while((s32[]{:T(128)}, f32[4,3,256]{2,1,0:T(4,128)S(1)}, ...), condition=%wide.region_8.9_spmd.clone.clone, body=%wide.region_3.8_spmd.clone.clone.sunk | while | flops 212740864 | bytes 14332273 | solution.py:322
  232.6 5.2 conditional.12
  245.0 7.2 collective-permute-done.39
  252.3 18.2 %collective-permute-start.53 = (bf16[4,96,864]{2,1,0:T(8,128)(2,1)}, bf16[4,96,864]{2,1,0:T(8,128)(2,1)}, u32[]{:S(2)}, u32[]{:S(2)}) collective-permute-start(bf16[4,96,864]{2,1,0:T(8,128)(2,1)} %collective-permute-done.49), channel_id=1, source_target_pairs={{2,4},{4,6},{3,5},{5,7},{10,12},{12,14},{11,13},{13,15},{18,20},{2... | collective-permute-start | bytes 1990664 | tf_op jit(solution)/shard_map/ppermute | solution.py:99
  272.5 12.5 %while.49 = (s32[]{:T(128)}, f32[256,4,3,64]{0,3,2,1:T(8,128)S(1)}, s32[2]{0:T(128)}, s32[]{:T(128)}, bf16[1024,256]{0,1:T(8,128)(2,1)S(1)}, /*index=5*/s32[2]{0...) while((s32[]{:T(128)}, f32[256,4,3,64]{0,3,2,1:T(8,128)S(1)}, ...), condition=%wide.region_12.13_spmd.clone.clone, body=%wide.region_9.12_spmd.clone.clone.sunk | while | flops 409539328 | bytes 3830113 | solution.py:336
  275.7 6.2 conditional.13
  292.1 10.2 %collective-permute-done.40 = bf16[4,96,864]{2,1,0:T(8,128)(2,1)} collective-permute-done((bf16[4,96,864]{2,1,0:T(8,128)(2,1)}, bf16[4,96,864]{2,1,0:T(8,128)(2,1)}, u32[]{:S(2)}, u32[]{:S(2)}) %collective-permute-start.40) | collective-permute-done | bytes 663584 | tf_op jit(solution)/shard_map/ppermute | solution.py:103
  305.7 11.3 %collective-permute-done.52 = bf16[4,96,864]{2,1,0:T(8,128)(2,1)S(1)} collective-permute-done((bf16[4,96,864]{2,1,0:T(8,128)(2,1)}, bf16[4,96,864]{2,1,0:T(8,128)(2,1)S(1)}, u32[]{:S(2)}, u32[]{:S(2)}) %collective-permute-start.52) | collective-permute-done | bytes 663584 | tf_op jit(solution)/shard_map/ppermute | solution.py:103
  320.0 8.8 %collective-permute-done.46 = bf16[4,96,864]{2,1,0:T(8,128)(2,1)S(1)} collective-permute-done((bf16[4,96,864]{2,1,0:T(8,128)(2,1)}, bf16[4,96,864]{2,1,0:T(8,128)(2,1)S(1)}, u32[]{:S(2)}, u32[]{:S(2)}) %collective-permute-start.46) | collective-permute-done | bytes 663584 | tf_op jit(solution)/shard_map/ppermute | solution.py:103
  330.3 5.0 fusion.162
  342.8 10.8 %collective-permute-done.31 = bf16[256,1536]{1,0:T(8,128)(2,1)S(1)} collective-permute-done((bf16[256,1536]{1,0:T(8,128)(2,1)S(1)}, bf16[256,1536]{1,0:T(8,128)(2,1)S(1)}, u32[]{:S(2)}, u32[]{:S(2)}) %collective-permute-start.31) | collective-permute-done | bytes 786464 | tf_op jit(solution)/shard_map/ppermute | solution.py:83
  360.8 7.6 multiply_convert_fusion.1
  368.4 6.1 convolution_convert_fusion.1
  374.5 5.0 convolution_convert_fusion
  383.6 5.6 fusion.163
  409.7 6.0 convolution_convert_fusion.3
  424.2 6.0 add_convert_fusion
  436.9 30.6 %collective-permute-start.117 = (bf16[4,96,864]{2,1,0:T(8,128)(2,1)S(1)}, bf16[4,96,864]{2,1,0:T(8,128)(2,1)S(1)}, u32[]{:S(2)}, u32[]{:S(2)}) collective-permute-start(bf16[4,96,864]{2,1,0:T(8,128)(2,1)S(1)} %fusion.73), channel_id=1, source_target_pairs={{4,2},{6,4},{5,3},{7,5},{12,10},{14,12},{13,11},{15,13},{20,18},{2... | collective-permute-start | bytes 1990664 | tf_op jit(solution)/shard_map/ppermute | solution.py:136
  475.5 43.1 %collective-permute-start.120 = (bf16[4,96,864]{2,1,0:T(8,128)(2,1)S(1)}, bf16[4,96,864]{2,1,0:T(8,128)(2,1)S(1)}, u32[]{:S(2)}, u32[]{:S(2)}) collective-permute-start(bf16[4,96,864]{2,1,0:T(8,128)(2,1)S(1)} %get-tuple-element.688), channel_id=1, source_target_pairs={{0,2},{2,4},{1,3},{3,5},{8,10},{10,12},{9,11},{11,13},{16,18},{18,... | collective-permute-start | bytes 1990664 | tf_op jit(solution)/shard_map/ppermute | solution.py:130
  536.8 12.4 %collective-permute-done.111 = bf16[4,96,864]{2,1,0:T(8,128)(2,1)S(1)} collective-permute-done((bf16[4,96,864]{2,1,0:T(8,128)(2,1)S(1)}, bf16[4,96,864]{2,1,0:T(8,128)(2,1)S(1)}, u32[]{:S(2)}, u32[]{:S(2)}) %collective-permute-start.111) | collective-permute-done | bytes 663584 | tf_op jit(solution)/shard_map/ppermute | solution.py:130
  551.7 10.9 %collective-permute-done.102 = bf16[4,96,864]{2,1,0:T(8,128)(2,1)S(1)} collective-permute-done((bf16[4,96,864]{2,1,0:T(8,128)(2,1)S(1)}, bf16[4,96,864]{2,1,0:T(8,128)(2,1)S(1)}, u32[]{:S(2)}, u32[]{:S(2)}) %collective-permute-start.102) | collective-permute-done | bytes 663584 | tf_op jit(solution)/shard_map/ppermute | solution.py:130
  562.6 5.2 collective-permute-start.121
  580.7 16.0 %while.50 = (s32[]{:T(128)}, f32[256,4,3,64]{0,3,2,1:T(8,128)S(1)}, bf16[2,512,512]{1,2,0:T(8,128)(2,1)}, s32[2]{0:T(128)S(1)}, s32[]{:T(128)}, /*index=5*/bf16[...) while((s32[]{:T(128)}, f32[256,4,3,64]{0,3,2,1:T(8,128)S(1)}, ...), condition=%wide.region_18.19_spmd.clone.clone, body=%wide.region_15.18_spmd.clone.clone.sunk | while | flops 1024463616 | bytes 36410280 | solution.py:425
  583.4 9.1 %conditional.14 = (f32[256,4,3,64]{0,3,2,1:T(8,128)S(1)}, bf16[1,512,512]{1,2,0:T(8,128)(2,1)S(1)}) conditional(s32[]{:T(128)} %convert_element_type.1363, f32[256,4,3,64]{0,3,2,1:T(8,128)S(1)} %get-tuple-element.1150, (s32[]{:T(128)}, bf16[1024,256]{0,1:T(8,128)(2,1)S(1)}, s32[256]{0:T(256)S(1)}, s32[2]{0:T(128)S(1)}, s32[256]{0:T(256)S(1)}, ...), branch_computations={%region_16.16_spmd, %region_17.17_spmd} | conditional | flops 1024462080 | bytes 35357816 | solution.py:423
  618.8 13.2 %collective-permute-start.90 = (bf16[4,96,768]{2,1,0:T(8,128)(2,1)}, bf16[4,96,768]{2,1,0:T(8,128)(2,1)}, u32[]{:S(2)}, u32[]{:S(2)}) collective-permute-start(bf16[4,96,768]{2,1,0:T(8,128)(2,1)} %get-tuple-element.700), channel_id=1, source_target_pairs={{0,8},{8,0},{16,24},{24,16},{1,9},{9,1},{17,25},{25,17},{2,10},{10... | collective-permute-start | bytes 1769480 | tf_op jit(solution)/shard_map/ppermute | solution.py:83
  647.4 5.8 collective-permute-done.124
  667.1 5.2 collective-permute-done.115
  676.5 5.4 collective-permute-done.105
  682.6 5.9 collective-permute-done.106
  708.6 5.4 collective-permute-done.68
  727.6 5.1 collective-permute-start.95
  735.8 7.9 collective-permute-start.86
  747.3 7.5 collective-permute-start.96
  770.4 7.4 collective-permute-done.72
  (706 shorter events, 420.0 us)
Async XLA Ops:
  0.6 51.0 %collective-permute-start.22 = (bf16[96,768]{1,0:T(8,128)(2,1)}, bf16[96,768]{1,0:T(8,128)(2,1)}, u32[]{:S(2)}, u32[]{:S(2)}) collective-permute-start(bf16[96,768]{1,0:T(8,128)(2,1)} %bitcast.746), channel_id=1, source_target_pairs={{2,0},{4,2},{6,4},{3,1},{5,3},{7,5},{10,8},{12,10},{14,12},{11,9},... | collective-permute-start | bytes 442376 | tf_op jit(solution)/shard_map/ppermute | solution.py:103
  1.9 59.1 %collective-permute-start.21 = (bf16[96,768]{1,0:T(8,128)(2,1)}, bf16[96,768]{1,0:T(8,128)(2,1)}, u32[]{:S(2)}, u32[]{:S(2)}) collective-permute-start(bf16[96,768]{1,0:T(8,128)(2,1)} %bitcast.747), channel_id=1, source_target_pairs={{0,2},{2,4},{4,6},{1,3},{3,5},{5,7},{8,10},{10,12},{12,14},{9,11},... | collective-permute-start | bytes 442376 | tf_op jit(solution)/shard_map/ppermute | solution.py:99
  10.4 32.4 %collective-permute-start.1 = (bf16[112,512]{1,0:T(8,128)(2,1)}, bf16[112,512]{1,0:T(8,128)(2,1)}, u32[]{:S(2)}, u32[]{:S(2)}) collective-permute-start(bf16[112,512]{1,0:T(8,128)(2,1)} %fusion.138), channel_id=1, source_target_pairs={{2,0},{4,2},{6,4},{3,1},{5,3},{7,5},{10,8},{12,10},{14,12},{11,9},... | collective-permute-start | bytes 344072 | tf_op jit(solution)/shard_map/ppermute | solution.py:103
  11.7 36.7 %collective-permute-start = (bf16[112,512]{1,0:T(8,128)(2,1)}, bf16[112,512]{1,0:T(8,128)(2,1)}, u32[]{:S(2)}, u32[]{:S(2)}) collective-permute-start(bf16[112,512]{1,0:T(8,128)(2,1)} %fusion.138), channel_id=1, source_target_pairs={{0,2},{2,4},{4,6},{1,3},{3,5},{5,7},{8,10},{10,12},{12,14},{9,11},... | collective-permute-start | bytes 344072 | tf_op jit(solution)/shard_map/ppermute | solution.py:99
  16.9 54.2 %collective-permute-start.13 = (bf16[96,768]{1,0:T(8,128)(2,1)}, bf16[96,768]{1,0:T(8,128)(2,1)}, u32[]{:S(2)}, u32[]{:S(2)}) collective-permute-start(bf16[96,768]{1,0:T(8,128)(2,1)} %param.34), channel_id=1, source_target_pairs={{2,0},{4,2},{6,4},{3,1},{5,3},{7,5},{10,8},{12,10},{14,12},{11,9},... | collective-permute-start | bytes 442376 | tf_op jit(solution)/shard_map/ppermute | solution.py:103
  61.1 64.6 %collective-permute-start.59 = (bf16[256,1536]{1,0:T(8,128)(2,1)}, bf16[256,1536]{1,0:T(8,128)(2,1)}, u32[]{:S(2)}, u32[]{:S(2)}) collective-permute-start(bf16[256,1536]{1,0:T(8,128)(2,1)} %bitcast.130), channel_id=1, source_target_pairs={{0,16},{8,24},{16,0},{24,8},{1,17},{9,25},{17,1},{25,9},{2,18},{10... | collective-permute-start | bytes 2359304 | tf_op jit(solution)/shard_map/ppermute | solution.py:83
  71.1 57.0 %collective-permute-start.60 = (bf16[256,1536]{1,0:T(8,128)(2,1)}, bf16[256,1536]{1,0:T(8,128)(2,1)S(1)}, u32[]{:S(2)}, u32[]{:S(2)}) collective-permute-start(bf16[256,1536]{1,0:T(8,128)(2,1)} %bitcast.130), channel_id=1, source_target_pairs={{0,8},{8,0},{16,24},{24,16},{1,9},{9,1},{17,25},{25,17},{2,10},{10... | collective-permute-start | bytes 2359304 | tf_op jit(solution)/shard_map/ppermute | solution.py:83
  130.8 36.5 %collective-permute-start.19 = (bf16[4,96,768]{2,1,0:T(8,128)(2,1)}, bf16[4,96,768]{2,1,0:T(8,128)(2,1)}, u32[]{:S(2)}, u32[]{:S(2)}) collective-permute-start(bf16[4,96,768]{2,1,0:T(8,128)(2,1)} %bitcast_dynamic-update-slice_fusion.51), channel_id=1, source_target_pairs={{0,8},{8,0},{16,24},{24,16},{1,9},{9,1},{17,25},{25,17},{2,10},{10... | collective-permute-start | bytes 1769480 | tf_op jit(solution)/shard_map/ppermute | solution.py:83
  131.0 81.8 %collective-permute-start.38 = (bf16[4,96,864]{2,1,0:T(8,128)(2,1)}, bf16[4,96,864]{2,1,0:T(8,128)(2,1)}, u32[]{:S(2)}, u32[]{:S(2)}) collective-permute-start(bf16[4,96,864]{2,1,0:T(8,128)(2,1)} %get-tuple-element.704), channel_id=1, source_target_pairs={{2,0},{4,2},{6,4},{3,1},{5,3},{7,5},{10,8},{12,10},{14,12},{11,9},... | collective-permute-start | bytes 1990664 | tf_op jit(solution)/shard_map/ppermute | solution.py:103
  136.9 91.1 %collective-permute-start.37 = (bf16[4,96,864]{2,1,0:T(8,128)(2,1)}, bf16[4,96,864]{2,1,0:T(8,128)(2,1)}, u32[]{:S(2)}, u32[]{:S(2)}) collective-permute-start(bf16[4,96,864]{2,1,0:T(8,128)(2,1)} %get-tuple-element.704), channel_id=1, source_target_pairs={{0,2},{2,4},{4,6},{1,3},{3,5},{5,7},{8,10},{10,12},{12,14},{9,11},... | collective-permute-start | bytes 1990664 | tf_op jit(solution)/shard_map/ppermute | solution.py:99
  149.2 34.1 %collective-permute-start.61 = (bf16[256,1536]{1,0:T(8,128)(2,1)}, bf16[256,1536]{1,0:T(8,128)(2,1)}, u32[]{:S(2)}, u32[]{:S(2)}) collective-permute-start(bf16[256,1536]{1,0:T(8,128)(2,1)} %collective-permute-done.59), channel_id=1, source_target_pairs={{0,8},{8,0},{16,24},{24,16},{1,9},{9,1},{17,25},{25,17},{2,10},{10... | collective-permute-start | bytes 2359304 | tf_op jit(solution)/shard_map/ppermute | solution.py:83
  150.3 36.3 %collective-permute-start.20 = (bf16[4,96,768]{2,1,0:T(8,128)(2,1)}, bf16[4,96,768]{2,1,0:T(8,128)(2,1)}, u32[]{:S(2)}, u32[]{:S(2)}) collective-permute-start(bf16[4,96,768]{2,1,0:T(8,128)(2,1)} %collective-permute-done.18), channel_id=1, source_target_pairs={{0,8},{8,0},{16,24},{24,16},{1,9},{9,1},{17,25},{25,17},{2,10},{10... | collective-permute-start | bytes 1769480 | tf_op jit(solution)/shard_map/ppermute | solution.py:83
  183.3 46.1 %collective-permute-start.44 = (bf16[4,96,864]{2,1,0:T(8,128)(2,1)}, bf16[4,96,864]{2,1,0:T(8,128)(2,1)}, u32[]{:S(2)}, u32[]{:S(2)}) collective-permute-start(bf16[4,96,864]{2,1,0:T(8,128)(2,1)} %get-tuple-element.705), channel_id=1, source_target_pairs={{2,0},{4,2},{6,4},{3,1},{5,3},{7,5},{10,8},{12,10},{14,12},{11,9},... | collective-permute-start | bytes 1990664 | tf_op jit(solution)/shard_map/ppermute | solution.py:103
  186.6 55.5 %collective-permute-start.43 = (bf16[4,96,864]{2,1,0:T(8,128)(2,1)}, bf16[4,96,864]{2,1,0:T(8,128)(2,1)}, u32[]{:S(2)}, u32[]{:S(2)}) collective-permute-start(bf16[4,96,864]{2,1,0:T(8,128)(2,1)} %get-tuple-element.705), channel_id=1, source_target_pairs={{0,2},{2,4},{4,6},{1,3},{3,5},{5,7},{8,10},{10,12},{12,14},{9,11},... | collective-permute-start | bytes 1990664 | tf_op jit(solution)/shard_map/ppermute | solution.py:99
  203.9 36.3 %collective-permute-start.50 = (bf16[4,96,864]{2,1,0:T(8,128)(2,1)}, bf16[4,96,864]{2,1,0:T(8,128)(2,1)}, u32[]{:S(2)}, u32[]{:S(2)}) collective-permute-start(bf16[4,96,864]{2,1,0:T(8,128)(2,1)} %get-tuple-element.703), channel_id=1, source_target_pairs={{2,0},{4,2},{6,4},{3,1},{5,3},{7,5},{10,8},{12,10},{14,12},{11,9},... | collective-permute-start | bytes 1990664 | tf_op jit(solution)/shard_map/ppermute | solution.py:103
  229.4 41.1 %collective-permute-start.41 = (bf16[4,96,864]{2,1,0:T(8,128)(2,1)}, bf16[4,96,864]{2,1,0:T(8,128)(2,1)S(1)}, u32[]{:S(2)}, u32[]{:S(2)}) collective-permute-start(bf16[4,96,864]{2,1,0:T(8,128)(2,1)} %collective-permute-done.37), channel_id=1, source_target_pairs={{2,4},{4,6},{3,5},{5,7},{10,12},{12,14},{11,13},{13,15},{18,20},{2... | collective-permute-start | bytes 1990664 | tf_op jit(solution)/shard_map/ppermute | solution.py:99
  240.2 44.9 %collective-permute-start.51 = (bf16[4,96,864]{2,1,0:T(8,128)(2,1)}, bf16[4,96,864]{2,1,0:T(8,128)(2,1)}, u32[]{:S(2)}, u32[]{:S(2)}) collective-permute-start(bf16[4,96,864]{2,1,0:T(8,128)(2,1)} %collective-permute-done.50), channel_id=1, source_target_pairs={{2,0},{4,2},{3,1},{5,3},{10,8},{12,10},{11,9},{13,11},{18,16},{20,... | collective-permute-start | bytes 1990664 | tf_op jit(solution)/shard_map/ppermute | solution.py:103
  242.2 47.1 %collective-permute-start.45 = (bf16[4,96,864]{2,1,0:T(8,128)(2,1)}, bf16[4,96,864]{2,1,0:T(8,128)(2,1)}, u32[]{:S(2)}, u32[]{:S(2)}) collective-permute-start(bf16[4,96,864]{2,1,0:T(8,128)(2,1)} %collective-permute-done.44), channel_id=1, source_target_pairs={{2,0},{4,2},{3,1},{5,3},{10,8},{12,10},{11,9},{13,11},{18,16},{20,... | collective-permute-start | bytes 1990664 | tf_op jit(solution)/shard_map/ppermute | solution.py:103
  243.5 46.6 %collective-permute-start.47 = (bf16[4,96,864]{2,1,0:T(8,128)(2,1)}, bf16[4,96,864]{2,1,0:T(8,128)(2,1)}, u32[]{:S(2)}, u32[]{:S(2)}) collective-permute-start(bf16[4,96,864]{2,1,0:T(8,128)(2,1)} %collective-permute-done.43), channel_id=1, source_target_pairs={{2,4},{4,6},{3,5},{5,7},{10,12},{12,14},{11,13},{13,15},{18,20},{2... | collective-permute-start | bytes 1990664 | tf_op jit(solution)/shard_map/ppermute | solution.py:99
  252.3 39.1 %collective-permute-start.53 = (bf16[4,96,864]{2,1,0:T(8,128)(2,1)}, bf16[4,96,864]{2,1,0:T(8,128)(2,1)}, u32[]{:S(2)}, u32[]{:S(2)}) collective-permute-start(bf16[4,96,864]{2,1,0:T(8,128)(2,1)} %collective-permute-done.49), channel_id=1, source_target_pairs={{2,4},{4,6},{3,5},{5,7},{10,12},{12,14},{11,13},{13,15},{18,20},{2... | collective-permute-start | bytes 1990664 | tf_op jit(solution)/shard_map/ppermute | solution.py:99
  270.4 31.9 %collective-permute-start.40 = (bf16[4,96,864]{2,1,0:T(8,128)(2,1)}, bf16[4,96,864]{2,1,0:T(8,128)(2,1)}, u32[]{:S(2)}, u32[]{:S(2)}) collective-permute-start(bf16[4,96,864]{2,1,0:T(8,128)(2,1)} %collective-permute-done.39), channel_id=1, source_target_pairs={{2,0},{3,1},{10,8},{11,9},{18,16},{19,17},{26,24},{27,25}} | collective-permute-start | bytes 1990664 | tf_op jit(solution)/shard_map/ppermute | solution.py:103
  289.2 50.3 %collective-permute-start.42 = (bf16[4,96,864]{2,1,0:T(8,128)(2,1)S(1)}, bf16[4,96,864]{2,1,0:T(8,128)(2,1)S(1)}, u32[]{:S(2)}, u32[]{:S(2)}) collective-permute-start(bf16[4,96,864]{2,1,0:T(8,128)(2,1)S(1)} %copy-done.55), channel_id=1, source_target_pairs={{4,6},{5,7},{12,14},{13,15},{20,22},{21,23},{28,30},{29,31}} | collective-permute-start | bytes 1990664 | tf_op jit(solution)/shard_map/ppermute | solution.py:99
  290.1 38.7 %collective-permute-start.46 = (bf16[4,96,864]{2,1,0:T(8,128)(2,1)}, bf16[4,96,864]{2,1,0:T(8,128)(2,1)S(1)}, u32[]{:S(2)}, u32[]{:S(2)}) collective-permute-start(bf16[4,96,864]{2,1,0:T(8,128)(2,1)} %collective-permute-done.45), channel_id=1, source_target_pairs={{2,0},{3,1},{10,8},{11,9},{18,16},{19,17},{26,24},{27,25}} | collective-permute-start | bytes 1990664 | tf_op jit(solution)/shard_map/ppermute | solution.py:103
  291.4 49.5 %collective-permute-start.48 = (bf16[4,96,864]{2,1,0:T(8,128)(2,1)}, bf16[4,96,864]{2,1,0:T(8,128)(2,1)S(1)}, u32[]{:S(2)}, u32[]{:S(2)}) collective-permute-start(bf16[4,96,864]{2,1,0:T(8,128)(2,1)} %collective-permute-done.47), channel_id=1, source_target_pairs={{4,6},{5,7},{12,14},{13,15},{20,22},{21,23},{28,30},{29,31}} | collective-permute-start | bytes 1990664 | tf_op jit(solution)/shard_map/ppermute | solution.py:99
  396.3 34.1 %collective-permute-start.116 = (bf16[4,96,864]{2,1,0:T(8,128)(2,1)}, bf16[4,96,864]{2,1,0:T(8,128)(2,1)}, u32[]{:S(2)}, u32[]{:S(2)}) collective-permute-start(bf16[4,96,864]{2,1,0:T(8,128)(2,1)} %get-tuple-element.689), channel_id=1, source_target_pairs={{6,4},{7,5},{14,12},{15,13},{22,20},{23,21},{30,28},{31,29}} | collective-permute-start | bytes 1990664 | tf_op jit(solution)/shard_map/ppermute | solution.py:136
  397.8 69.9 %collective-permute-start.119 = (bf16[4,96,864]{2,1,0:T(8,128)(2,1)}, bf16[4,96,864]{2,1,0:T(8,128)(2,1)}, u32[]{:S(2)}, u32[]{:S(2)}) collective-permute-start(bf16[4,96,864]{2,1,0:T(8,128)(2,1)} %get-tuple-element.690), channel_id=1, source_target_pairs={{0,2},{1,3},{8,10},{9,11},{16,18},{17,19},{24,26},{25,27}} | collective-permute-start | bytes 1990664 | tf_op jit(solution)/shard_map/ppermute | solution.py:130
  430.4 39.0 %collective-permute-start.110 = (bf16[4,96,864]{2,1,0:T(8,128)(2,1)S(1)}, bf16[4,96,864]{2,1,0:T(8,128)(2,1)S(1)}, u32[]{:S(2)}, u32[]{:S(2)}) collective-permute-start(bf16[4,96,864]{2,1,0:T(8,128)(2,1)S(1)} %get-tuple-element.694), channel_id=1, source_target_pairs={{0,2},{1,3},{8,10},{9,11},{16,18},{17,19},{24,26},{25,27}} | collective-permute-start | bytes 1990664 | tf_op jit(solution)/shard_map/ppermute | solution.py:130
  433.3 35.2 %collective-permute-start.63 = (bf16[256,1536]{1,0:T(8,128)(2,1)S(1)}, bf16[256,1536]{1,0:T(8,128)(2,1)S(1)}, u32[]{:S(2)}, u32[]{:S(2)}) collective-permute-start(bf16[256,1536]{1,0:T(8,128)(2,1)S(1)} %get-tuple-element.684), channel_id=1, source_target_pairs={{0,8},{8,0},{16,24},{24,16},{1,9},{9,1},{17,25},{25,17},{2,10},{10... | collective-permute-start | bytes 2359304 | tf_op jit(solution)/shard_map/ppermute | solution.py:83
  435.4 39.8 %collective-permute-start.101 = (bf16[4,96,864]{2,1,0:T(8,128)(2,1)S(1)}, bf16[4,96,864]{2,1,0:T(8,128)(2,1)S(1)}, u32[]{:S(2)}, u32[]{:S(2)}) collective-permute-start(bf16[4,96,864]{2,1,0:T(8,128)(2,1)S(1)} %get-tuple-element.698), channel_id=1, source_target_pairs={{0,2},{1,3},{8,10},{9,11},{16,18},{17,19},{24,26},{25,27}} | collective-permute-start | bytes 1990664 | tf_op jit(solution)/shard_map/ppermute | solution.py:130
  436.9 32.9 %collective-permute-start.117 = (bf16[4,96,864]{2,1,0:T(8,128)(2,1)S(1)}, bf16[4,96,864]{2,1,0:T(8,128)(2,1)S(1)}, u32[]{:S(2)}, u32[]{:S(2)}) collective-permute-start(bf16[4,96,864]{2,1,0:T(8,128)(2,1)S(1)} %fusion.73), channel_id=1, source_target_pairs={{4,2},{6,4},{5,3},{7,5},{12,10},{14,12},{13,11},{15,13},{20,18},{2... | collective-permute-start | bytes 1990664 | tf_op jit(solution)/shard_map/ppermute | solution.py:136
  469.4 50.5 %collective-permute-start.62 = (bf16[256,1536]{1,0:T(8,128)(2,1)S(1)}, bf16[256,1536]{1,0:T(8,128)(2,1)S(1)}, u32[]{:S(2)}, u32[]{:S(2)}) collective-permute-start(bf16[256,1536]{1,0:T(8,128)(2,1)S(1)} %get-tuple-element.683), channel_id=1, source_target_pairs={{0,8},{8,0},{16,24},{24,16},{1,9},{9,1},{17,25},{25,17},{2,10},{10... | collective-permute-start | bytes 2359304 | tf_op jit(solution)/shard_map/ppermute | solution.py:83
  469.8 51.3 %collective-permute-start.64 = (bf16[256,1536]{1,0:T(8,128)(2,1)S(1)}, bf16[256,1536]{1,0:T(8,128)(2,1)S(1)}, u32[]{:S(2)}, u32[]{:S(2)}) collective-permute-start(bf16[256,1536]{1,0:T(8,128)(2,1)S(1)} %fusion.64), channel_id=1, source_target_pairs={{0,16},{8,24},{16,0},{24,8},{1,17},{9,25},{17,1},{25,9},{2,18},{10... | collective-permute-start | bytes 2359304 | tf_op jit(solution)/shard_map/ppermute | solution.py:83
  473.9 52.2 %collective-permute-start.55 = (bf16[256,1536]{1,0:T(8,128)(2,1)S(1)}, bf16[256,1536]{1,0:T(8,128)(2,1)S(1)}, u32[]{:S(2)}, u32[]{:S(2)}) collective-permute-start(bf16[256,1536]{1,0:T(8,128)(2,1)S(1)} %get-tuple-element.685), channel_id=1, source_target_pairs={{0,8},{8,0},{16,24},{24,16},{1,9},{9,1},{17,25},{25,17},{2,10},{10... | collective-permute-start | bytes 2359304 | tf_op jit(solution)/shard_map/ppermute | solution.py:83
  475.2 54.2 %collective-permute-start.57 = (bf16[256,1536]{1,0:T(8,128)(2,1)S(1)}, bf16[256,1536]{1,0:T(8,128)(2,1)S(1)}, u32[]{:S(2)}, u32[]{:S(2)}) collective-permute-start(bf16[256,1536]{1,0:T(8,128)(2,1)S(1)} %fusion.67), channel_id=1, source_target_pairs={{0,16},{8,24},{16,0},{24,8},{1,17},{9,25},{17,1},{25,9},{2,18},{10... | collective-permute-start | bytes 2359304 | tf_op jit(solution)/shard_map/ppermute | solution.py:83
  475.5 58.9 %collective-permute-start.120 = (bf16[4,96,864]{2,1,0:T(8,128)(2,1)S(1)}, bf16[4,96,864]{2,1,0:T(8,128)(2,1)S(1)}, u32[]{:S(2)}, u32[]{:S(2)}) collective-permute-start(bf16[4,96,864]{2,1,0:T(8,128)(2,1)S(1)} %get-tuple-element.688), channel_id=1, source_target_pairs={{0,2},{2,4},{1,3},{3,5},{8,10},{10,12},{9,11},{11,13},{16,18},{18,... | collective-permute-start | bytes 1990664 | tf_op jit(solution)/shard_map/ppermute | solution.py:130
  519.9 94.4 %collective-permute-start.118 = (bf16[4,96,864]{2,1,0:T(8,128)(2,1)}, bf16[4,96,864]{2,1,0:T(8,128)(2,1)}, u32[]{:S(2)}, u32[]{:S(2)}) collective-permute-start(bf16[4,96,864]{2,1,0:T(8,128)(2,1)} %get-tuple-element.687), channel_id=1, source_target_pairs={{2,0},{4,2},{6,4},{3,1},{5,3},{7,5},{10,8},{12,10},{14,12},{11,9},... | collective-permute-start | bytes 1990664 | tf_op jit(solution)/shard_map/ppermute | solution.py:136
  526.1 36.5 %collective-permute-start.102 = (bf16[4,96,864]{2,1,0:T(8,128)(2,1)S(1)}, bf16[4,96,864]{2,1,0:T(8,128)(2,1)S(1)}, u32[]{:S(2)}, u32[]{:S(2)}) collective-permute-start(bf16[4,96,864]{2,1,0:T(8,128)(2,1)S(1)} %get-tuple-element.696), channel_id=1, source_target_pairs={{0,2},{2,4},{1,3},{3,5},{8,10},{10,12},{9,11},{11,13},{16,18},{18,... | collective-permute-start | bytes 1990664 | tf_op jit(solution)/shard_map/ppermute | solution.py:130
  529.5 39.4 %collective-permute-start.65 = (bf16[256,1536]{1,0:T(8,128)(2,1)S(1)}, bf16[256,1536]{1,0:T(8,128)(2,1)S(1)}, u32[]{:S(2)}, u32[]{:S(2)}) collective-permute-start(bf16[256,1536]{1,0:T(8,128)(2,1)S(1)} %fusion.66), channel_id=1, source_target_pairs={{0,1},{1,0},{2,3},{3,2},{4,5},{5,4},{6,7},{7,6},{8,9},{9,8},{10,11... | collective-permute-start | bytes 2359304 | tf_op jit(solution)/shard_map/ppermute | solution.py:87
  534.4 99.5 %collective-permute-start.109 = (bf16[4,96,864]{2,1,0:T(8,128)(2,1)}, bf16[4,96,864]{2,1,0:T(8,128)(2,1)}, u32[]{:S(2)}, u32[]{:S(2)}) collective-permute-start(bf16[4,96,864]{2,1,0:T(8,128)(2,1)} %get-tuple-element.691), channel_id=1, source_target_pairs={{2,0},{4,2},{6,4},{3,1},{5,3},{7,5},{10,8},{12,10},{14,12},{11,9},... | collective-permute-start | bytes 1990664 | tf_op jit(solution)/shard_map/ppermute | solution.py:136
  562.6 56.2 %collective-permute-start.121 = (bf16[4,96,864]{2,1,0:T(8,128)(2,1)}, bf16[4,96,864]{2,1,0:T(8,128)(2,1)}, u32[]{:S(2)}, u32[]{:S(2)}) collective-permute-start(bf16[4,96,864]{2,1,0:T(8,128)(2,1)} %fusion.72), channel_id=1, source_target_pairs={{0,2},{2,4},{4,6},{1,3},{3,5},{5,7},{8,10},{10,12},{12,14},{9,11},... | collective-permute-start | bytes 1990664 | tf_op jit(solution)/shard_map/ppermute | solution.py:130
  568.8 65.6 %collective-permute-start.112 = (bf16[4,96,864]{2,1,0:T(8,128)(2,1)}, bf16[4,96,864]{2,1,0:T(8,128)(2,1)}, u32[]{:S(2)}, u32[]{:S(2)}) collective-permute-start(bf16[4,96,864]{2,1,0:T(8,128)(2,1)} %fusion.78), channel_id=1, source_target_pairs={{0,2},{2,4},{4,6},{1,3},{3,5},{5,7},{8,10},{10,12},{12,14},{9,11},... | collective-permute-start | bytes 1990664 | tf_op jit(solution)/shard_map/ppermute | solution.py:130
  618.8 83.5 %collective-permute-start.90 = (bf16[4,96,768]{2,1,0:T(8,128)(2,1)}, bf16[4,96,768]{2,1,0:T(8,128)(2,1)}, u32[]{:S(2)}, u32[]{:S(2)}) collective-permute-start(bf16[4,96,768]{2,1,0:T(8,128)(2,1)} %get-tuple-element.700), channel_id=1, source_target_pairs={{0,8},{8,0},{16,24},{24,16},{1,9},{9,1},{17,25},{25,17},{2,10},{10... | collective-permute-start | bytes 1769480 | tf_op jit(solution)/shard_map/ppermute | solution.py:83
  634.0 91.2 %collective-permute-start.89 = (bf16[4,96,768]{2,1,0:T(8,128)(2,1)}, bf16[4,96,768]{2,1,0:T(8,128)(2,1)}, u32[]{:S(2)}, u32[]{:S(2)}) collective-permute-start(bf16[4,96,768]{2,1,0:T(8,128)(2,1)} %get-tuple-element.699), channel_id=1, source_target_pairs={{0,8},{8,0},{16,24},{24,16},{1,9},{9,1},{17,25},{25,17},{2,10},{10... | collective-permute-start | bytes 1769480 | tf_op jit(solution)/shard_map/ppermute | solution.py:83
  634.4 71.3 %collective-permute-start.81 = (bf16[4,96,768]{2,1,0:T(8,128)(2,1)}, bf16[4,96,768]{2,1,0:T(8,128)(2,1)}, u32[]{:S(2)}, u32[]{:S(2)}) collective-permute-start(bf16[4,96,768]{2,1,0:T(8,128)(2,1)} %get-tuple-element.702), channel_id=1, source_target_pairs={{0,8},{8,0},{16,24},{24,16},{1,9},{9,1},{17,25},{25,17},{2,10},{10... | collective-permute-start | bytes 1769480 | tf_op jit(solution)/shard_map/ppermute | solution.py:83
  636.3 96.3 %collective-permute-start.80 = (bf16[4,96,768]{2,1,0:T(8,128)(2,1)}, bf16[4,96,768]{2,1,0:T(8,128)(2,1)}, u32[]{:S(2)}, u32[]{:S(2)}) collective-permute-start(bf16[4,96,768]{2,1,0:T(8,128)(2,1)} %get-tuple-element.701), channel_id=1, source_target_pairs={{0,8},{8,0},{16,24},{24,16},{1,9},{9,1},{17,25},{25,17},{2,10},{10... | collective-permute-start | bytes 1769480 | tf_op jit(solution)/shard_map/ppermute | solution.py:83
  721.8 34.3 %collective-permute-start.69 = (bf16[256,1536]{1,0:T(8,128)(2,1)S(1)}, bf16[256,1536]{1,0:T(8,128)(2,1)}, u32[]{:S(2)}, u32[]{:S(2)}) collective-permute-start(bf16[256,1536]{1,0:T(8,128)(2,1)S(1)} %get-tuple-element.788), channel_id=1, source_target_pairs={{0,1},{1,0},{2,3},{3,2},{4,5},{5,4},{6,7},{7,6},{8,9},{9,8},{10,11... | collective-permute-start | bytes 2359304 | tf_op jit(solution)/shard_map/ppermute | solution.py:87
  754.8 40.4 %collective-permute-start.94 = (bf16[96,768]{1,0:T(8,128)(2,1)S(1)}, bf16[96,768]{1,0:T(8,128)(2,1)S(1)}, u32[]{:S(2)}, u32[]{:S(2)}) collective-permute-start(bf16[96,768]{1,0:T(8,128)(2,1)S(1)} %get-tuple-element.746), channel_id=1, source_target_pairs={{2,0},{4,2},{6,4},{3,1},{5,3},{7,5},{10,8},{12,10},{14,12},{11,9},... | collective-permute-start | bytes 442376 | tf_op jit(solution)/shard_map/ppermute | solution.py:136
  769.0 33.6 %collective-permute-start.85 = (bf16[96,768]{1,0:T(8,128)(2,1)S(1)}, bf16[96,768]{1,0:T(8,128)(2,1)S(1)}, u32[]{:S(2)}, u32[]{:S(2)}) collective-permute-start(bf16[96,768]{1,0:T(8,128)(2,1)S(1)} %get-tuple-element.750), channel_id=1, source_target_pairs={{2,0},{4,2},{6,4},{3,1},{5,3},{7,5},{10,8},{12,10},{14,12},{11,9},... | collective-permute-start | bytes 442376 | tf_op jit(solution)/shard_map/ppermute | solution.py:136
  (169 other events, 2193.9 us)
